TPU v7x, 512 devices: a whole 4x8x8 slice. The times are simulated.
512 devices in a mesh: ctx: 128 (over y, x, z_lo), head: 4 (over z_hi, core).
Axes of the slice: x: 4, y: 8, z: 8 (z_hi: 2, z_lo: 4; z = z_hi * 4 + z_lo), core: 2. Of those that a mesh axis runs over, the one named last changes fastest.
Arguments:
- q_nope: bfloat16 [16384, 8192], P('ctx', 'head'), may hold values from -480 to 480
- q_rope: bfloat16 [16384, 4096], P('ctx', 'head'), may hold values from -6 to 6
- latent: bfloat16 [16384, 512], P('ctx'), may hold values from -6 to 6
- key_rope: bfloat16 [16384, 64], P('ctx'), may hold values from -6 to 6
- w_key: bfloat16 [512, 8192], P('ctx', 'head'), may hold values from -0.25 to 0.25
- w_value: bfloat16 [512, 8192], P('ctx', 'head'), may hold values from -0.25 to 0.25
- stripe: int32 [16384], replicated, may hold values from 0 to 16383, as said below
- frame_len: int32 [129], replicated, may hold values from 1 to 254, as said below
- out_grad: bfloat16 [16384, 8192], P('ctx', 'head'), may hold values from -6 to 6
Outputs:
- attended: bfloat16 [16384, 8192], P('ctx', 'head')
- dq_nope: float32 [16384, 8192], P('ctx', 'head')
- dq_rope: float32 [16384, 4096], P('ctx', 'head')
- d_latent: float32 [16384, 512], P('ctx')
- d_key_rope: float32 [16384, 64], P('ctx')
Inputs may be any that keep to these rules, and one draw needn't show every extreme that they name: `stripe`: rows c * 128 to (c + 1) * 128 - 1 hold the episode positions c * 128 to (c + 1) * 128 - 1 in some order, each once. `frame_len`: frame 0 starts at position 0; every later frame k starts at (k - 1) * 128 + u with 1 <= u <= 127; the lengths sum to 16384.
All inputs are finite; a program needn't handle non-finite values.
Results may differ from a plain program's by a relative error of at most 0.028.
The roundings to bfloat16 on the way count: a program that leaves them out, or rounds other values in their place, can miss the bound.
Values may be sent and summed in bfloat16 or wider, within the bound.
A program may use at most 64 MiB of HBM per device.

v0:
```python
import jax
import jax.numpy as jnp
from jax import lax
from jax.sharding import PartitionSpec as P

HEAD_QK = 192
WINDOW = 128


masked_score = -1e30


def extended(block, sides, width):
    for axis, dim in sides:
        count = lax.axis_size(axis)
        forward = [(i, i + 1) for i in range(count - 1)]
        backward = [(target, source) for source, target in forward]
        low = lax.ppermute(
            lax.slice_in_dim(block, block.shape[dim] - width, None, axis=dim), axis, forward
        )
        high = lax.ppermute(lax.slice_in_dim(block, 0, width, axis=dim), axis, backward)
        block = jnp.concatenate([low, block, high], axis=dim)
    return block


def shifted(value, axis, steps):
    count = lax.axis_size(axis)
    initial, last = (max(0, -steps), min(count, count - steps))
    return lax.ppermute(value, axis, [(source, source + steps) for source in range(initial, last)])


def frames_of(positions, frame_len):
    starts = jnp.cumsum(frame_len) - frame_len
    return jnp.sum((starts[None, :] <= positions[:, None]).astype(jnp.int32), axis=1) - 1


def on_device(q_nope, q_rope, latent, key_rope, w_key, w_value, stripe, frame_len, out_grad):
    tok_rows, plain_cols = q_nope.shape
    latent_width = latent.shape[1]
    rope_width = key_rope.shape[1]
    head_count = q_rope.shape[1] // rope_width
    head_dim = plain_cols // head_count
    token_count = stripe.shape[0]
    window_rows = 3 * tok_rows
    softmax_scale = HEAD_QK ** (-0.5)
    place = lax.axis_index("ctx")
    padded_pos = jnp.concatenate(
        [jnp.zeros((tok_rows,), jnp.int32), stripe, jnp.zeros((tok_rows,), jnp.int32)]
    )
    window_start = place * tok_rows
    row_index = window_start + jnp.arange(window_rows, dtype=jnp.int32)
    key_valid = (row_index >= tok_rows) & (row_index < token_count + tok_rows)
    key_pos = lax.dynamic_slice_in_dim(padded_pos, window_start, window_rows)
    key_frame = frames_of(key_pos, frame_len)
    own_pos = key_pos[tok_rows : 2 * tok_rows]
    own_frame = key_frame[tok_rows : 2 * tok_rows]
    allowed = (
        key_valid[None, :]
        & (key_frame[None, :] <= own_frame[:, None])
        & (own_pos[:, None] - key_pos[None, :] < WINDOW)
    )
    key_weight, value_weight = (
        lax.all_gather(w_key, "ctx", axis=0, tiled=True),
        lax.all_gather(w_value, "ctx", axis=0, tiled=True),
    )
    joined = jnp.concatenate([latent, key_rope], axis=1)
    window = extended(joined, (("ctx", 0),), tok_rows)
    rot_win = window[:, latent_width:]
    source = window[:, :latent_width]
    keys_now = jnp.dot(source, key_weight, preferred_element_type=jnp.float32)
    values_now = jnp.dot(source, value_weight, preferred_element_type=jnp.float32)
    keys_win = keys_now.astype(jnp.bfloat16)
    values_win = values_now.astype(jnp.bfloat16)
    plain_q = q_nope.reshape(tok_rows, head_count, head_dim)
    rot_q = q_rope.reshape(tok_rows, head_count, rope_width)
    cotangent = out_grad.reshape(tok_rows, head_count, head_dim)
    keys_heads = keys_win.reshape(window_rows, head_count, head_dim)
    values_heads = values_win.reshape(window_rows, head_count, head_dim)
    scores = jnp.einsum("thd,khd->htk", plain_q, keys_heads, preferred_element_type=jnp.float32)
    scores = (
        scores + jnp.einsum("thr,kr->htk", rot_q, rot_win, preferred_element_type=jnp.float32)
    ) * softmax_scale
    scores = jnp.where(allowed[None], scores, masked_score)
    top_score = jnp.max(scores, axis=2, keepdims=True)
    total = jnp.sum(
        jnp.where(allowed[None], jnp.exp(scores - top_score), 0.0), axis=2, keepdims=True
    )
    lse = top_score + jnp.log(total)
    weights = jnp.where(allowed[None], jnp.exp(scores - lse), 0.0)
    probs = weights.astype(jnp.bfloat16)
    attended = jnp.einsum(
        "htk,khd->thd", probs, values_heads, preferred_element_type=jnp.float32
    ).astype(jnp.bfloat16)
    delta = jnp.sum(cotangent.astype(jnp.float32) * attended.astype(jnp.float32), axis=2).T
    prob_grad = jnp.einsum(
        "thd,khd->htk", cotangent, values_heads, preferred_element_type=jnp.float32
    )
    score_grad = (weights * (prob_grad - delta[:, :, None])).astype(jnp.bfloat16)
    grad_plain = softmax_scale * jnp.einsum(
        "htk,khd->thd", score_grad, keys_heads, preferred_element_type=jnp.float32
    )
    grad_rot = softmax_scale * jnp.einsum(
        "htk,kr->thr", score_grad, rot_win, preferred_element_type=jnp.float32
    )
    key_part = (
        (
            softmax_scale
            * jnp.einsum("htk,thd->khd", score_grad, plain_q, preferred_element_type=jnp.float32)
        )
        .astype(jnp.bfloat16)
        .reshape(window_rows, plain_cols)
    )
    value_part = (
        jnp.einsum("htk,thd->khd", probs, cotangent, preferred_element_type=jnp.float32)
        .astype(jnp.bfloat16)
        .reshape(window_rows, plain_cols)
    )
    rot_part = softmax_scale * jnp.einsum(
        "htk,thr->kr", score_grad, rot_q, preferred_element_type=jnp.float32
    )
    back_key, back_value = (key_weight, value_weight)
    contract = (((1,), (1,)), ((), ()))
    lat_part = lax.dot_general(key_part, back_key, contract, preferred_element_type=jnp.float32)
    lat_part = lat_part + lax.dot_general(
        value_part, back_value, contract, preferred_element_type=jnp.float32
    )
    joined_part = jnp.concatenate([lat_part, rot_part], axis=1)
    from_next = shifted(joined_part[:tok_rows], "ctx", -1)
    from_prev = shifted(joined_part[2 * tok_rows :], "ctx", 1)
    summed = joined_part[tok_rows : 2 * tok_rows] + from_next + from_prev
    lat_own = summed[:, :latent_width]
    rot_own = summed[:, latent_width:]
    d_latent, d_key_rope = lax.psum((lat_own, rot_own), "head")
    return (
        attended.reshape(tok_rows, plain_cols),
        grad_plain.reshape(tok_rows, plain_cols),
        grad_rot.reshape(tok_rows, head_count * rope_width),
        d_latent,
        d_key_rope,
    )


def solution(mesh):
    return jax.shard_map(
        on_device,
        mesh=mesh,
        in_specs=(
            P("ctx", "head"),
            P("ctx", "head"),
            P("ctx", None),
            P("ctx", None),
            P("ctx", "head"),
            P("ctx", "head"),
            P(),
            P(),
            P("ctx", "head"),
        ),
        out_specs=(
            P("ctx", "head"),
            P("ctx", "head"),
            P("ctx", "head"),
            P("ctx", None),
            P("ctx", None),
        ),
        check_vma=False,
    )
```

profile of v0, /device:TPU:1, one launch (start us, length us, event | category | flops | bytes accessed | tf_op | source)
XLA Modules:
  0.0 1504.2 jit_solution(5341373404443978194)
XLA Ops:
  10.5 1.3 collective-permute-start.1
  11.8 5.5 collective-permute-start
  21.3 1.3 copy.105
  23.3 592.7 %all-gather.5.cloned.1.call-done = bf16[128,4,2048]{2,1,0:T(4,128)(2,1)} async-done(((bf16[1,4,2048]{2,1,0:T(4,128)(2,1)}), bf16[128,4,2048]{2,1,0:T(4,128)(2,1)}) %all-gather.5.cloned.1.call-update) | async-done | bytes 2097168 | tf_op jit(solution)/shard_map/all_gather | solution.py:64
  616.0 3.9 reshape.159
  620.0 3.7 fusion.7
  623.7 677.0 %all-gather.7.cloned.1.call-done = bf16[128,4,2048]{2,1,0:T(4,128)(2,1)} async-done(((bf16[1,4,2048]{2,1,0:T(4,128)(2,1)}), bf16[128,4,2048]{2,1,0:T(4,128)(2,1)}) %all-gather.7.cloned.1.call-update) | async-done | bytes 2097168 | tf_op jit(solution)/shard_map/all_gather | solution.py:63
  1300.8 3.9 reshape.161
  1304.7 3.8 convolution_convert_fusion
  1308.5 1.9 copy.127
  1313.2 1.9 multiply_reduce_fusion
  1315.1 2.0 convolution_convert_fusion.2
  1317.1 2.1 fusion
  1319.2 1.2 fusion.13
  1320.4 2.0 multiply_convert_fusion
  1323.4 3.2 fusion.32
  1328.7 1.3 collective-permute-start.2
  1330.0 4.7 collective-permute-start.3
  1334.7 1.5 convolution_multiply_fusion
  1336.3 2.6 copy.117
  1340.8 1.1 fusion.19
  1344.1 107.4 %psum.15 = f32[128,64]{1,0:T(8,128)S(1)} all-reduce(f32[128,64]{1,0:T(8,128)S(1)} %slice.55), channel_id=1, replica_groups=mesh['ctx'=128,'head'=4] {'head'}, use_global_device_ids=true, to_apply=%region_7.8 | all-reduce | flops 8192 | bytes 65536 | tf_op jit(solution)/shard_map/psum | solution.py:133
  1452.3 43.7 %all-reduce.3.cloned.1.call-done = f32[128,512]{1,0:T(8,128)} async-done(((f32[128,512]{1,0:T(8,128)}), f32[128,512]{1,0:T(8,128)}) %all-reduce.3.cloned.1.call-update) | async-done | bytes 262160 | tf_op jit(solution)/shard_map/psum | solution.py:133
  1496.0 1.7 copy.143
  (70 shorter events, 18.4 us)
Async XLA Ops:
  7.2 16.0 %copy-start.11 = (bf16[128,64]{0,1:T(8,128)(2,1)S(1)}, bf16[128,64]{0,1:T(8,128)(2,1)}, u32[]{:S(2)}) copy-start(bf16[128,64]{0,1:T(8,128)(2,1)} %param.12) | copy-start | bytes 49156
  7.2 15.4 %copy-start.9 = (bf16[128,2048]{1,0:T(8,128)(2,1)S(1)}, bf16[128,2048]{1,0:T(8,128)(2,1)}, u32[]{:S(2)}) copy-start(bf16[128,2048]{1,0:T(8,128)(2,1)} %param.9) | copy-start | bytes 1572868
  7.2 608.8 %all-gather.5.cloned.1.call-start = ((), (), s32[]{:S(2)}) async-start(), calls=%async_computation.1 | async-start | bytes 2113536 | tf_op jit(solution)/shard_map/all_gather | solution.py:64
  7.9 1292.8 %all-gather.7.cloned.1.call-start = ((), (), s32[]{:S(2)}) async-start(), calls=%async_computation.2 | async-start | bytes 2113536 | tf_op jit(solution)/shard_map/all_gather | solution.py:63
  8.7 1487.3 %all-reduce.3.cloned.1.call-start = ((), (), s32[]{:S(2)}) async-start(), calls=%async_computation | async-start | bytes 524288 | tf_op jit(solution)/shard_map/psum | solution.py:133
  10.5 12.7 collective-permute-start.1
  11.8 11.4 collective-permute-start
  22.6 1292.4 %copy-start.5 = (bf16[128,2048]{0,1:T(8,128)(2,1)}, bf16[128,2048]{0,1:T(8,128)(2,1)S(1)}, u32[]{:S(2)}) copy-start(bf16[128,2048]{0,1:T(8,128)(2,1)S(1)} %copy.105) | copy-start | bytes 1572868
  22.9 1287.5 %copy-start = (bf16[128,2048]{0,1:T(8,128)(2,1)}, bf16[128,2048]{0,1:T(8,128)(2,1)S(1)}, u32[]{:S(2)}) copy-start(bf16[128,2048]{0,1:T(8,128)(2,1)S(1)} %copy.128) | copy-start | bytes 1572868
  1311.8 1.4 copy-start.12
  1319.1 1.3 copy-start.1
  1323.4 4.3 copy-start.6
  1323.4 3.3 copy-start.4
  1323.4 3.3 copy-start.8
  1327.7 8.5 copy-start.2
  1328.7 12.1 collective-permute-start.2
  1330.0 10.8 collective-permute-start.3
  1336.3 2.7 copy-start.10
  1336.3 4.6 copy-start.7
  1336.3 4.6 copy-start.3
Sparse Core Ops, SparseCore 0:
  10.1 605.8 all-gather.4
  618.1 682.6 all-gather.6
  1342.8 153.0 all-reduce.2
where the time goes:
time: 1510 us; the launch traced here: 1500 us
  waiting for transfers between devices  1320 us (87%)
  blocking collectives  107 us (7%)
  matrix products  24.3 us (2%)
  local copies, waits for them, and re-layouts  24 us (2%)
    all_gather x1, waiting for transfers between devices, on_device(): lax.all_gather(w_key, 'ctx', axis=0, tiled=True)  677 us
    all_gather x1, waiting for transfers between devices, on_device(): lax.all_gather(w_value, 'ctx', axis=0, tiled=True)  593 us
    psum x1, blocking collectives, on_device(): d_latent, d_key_rope = lax.psum((lat_own, rot_own), 'head')  107 us
    psum x1, waiting for transfers between devices, on_device(): d_latent, d_key_rope = lax.psum((lat_own, rot_own), 'head')  43.7 us
  transfers between devices with their start and end apart: 7, of which 4 were waited for; matrix products, arithmetic and copies ran while one was open for 2% of the time, Pallas kernels for 0%

commit v1 on v0

v1 whole, which is shorter than its diff:
```python
import jax
import jax.numpy as jnp
from jax import lax
from jax.experimental import pallas as pl
from jax.experimental.pallas import tpu as pltpu
from jax.sharding import PartitionSpec as P

HEAD_QK = 192
WINDOW = 128
SCALE = HEAD_QK ** (-0.5)
MASKED = -1e30

NY, NX, NZ = 8, 4, 4
TOK = 128
LATENT = 512
ROPE = 64
DIM = 128
PAIRS = 8
PAIR = 2 * DIM
JOINED = LATENT + 2 * ROPE
STAGES = 7
LAG = 2

BF16 = jnp.bfloat16
F32 = jnp.float32


def dot(a, b, ca, cb):
    return lax.dot_general(a, b, (((ca,), (cb,)), ((), ())), preferred_element_type=F32)


def kernel(
    q_hbm, qr_hbm, lat_ref, rope_ref, wk_ref, wv_ref, pos_ref, len_ref, o_hbm,
    att_hbm, dq_hbm, dqr_hbm, dlat_ref, drope_ref,
    q_buf, qr_buf, o_buf, att_buf, dq_buf, dqr_buf,
    pack, zbuf, mix, wk, wv, lat_win, rot_win, bias, acc,
    t1_src, t1_dst, t2_src, t2_dst, t3_src, t3_dst, t4, mine,
    in_sem, out_sem, z_send, z_recv, h_send, h_recv, c_send, c_recv, t_send, t_recv,
):
    me = lax.axis_index("ctx")
    head = lax.axis_index("head")
    z = lax.rem(me, NZ)
    x = lax.rem(lax.div(me, NZ), NX)
    y = lax.div(me, NZ * NX)
    core = lax.rem(head, 2)
    z_hi = lax.div(head, 2)

    def at(y_, x_, z_):
        return {"ctx": (y_ * NX + x_) * NZ + z_}

    z_peers = [lax.rem(z + d, NZ) for d in (1, 2, 3)]
    x_peers = [lax.rem(x + d, NX) for d in (1, 2, 3)]
    y_up, y_down = lax.rem(y + 1, NY), lax.rem(y + NY - 1, NY)
    x_up, x_down = x_peers[0], x_peers[2]
    tokens = NY * NX * NZ
    c_next, c_prev = lax.rem(me + 1, tokens), lax.rem(me + tokens - 1, tokens)
    sibling = {"head": z_hi * 2 + (1 - core)}
    partner = {"head": (1 - z_hi) * 2 + core}

    def remote(src, dst, send, recv, device):
        return pltpu.make_async_remote_copy(
            src_ref=src, dst_ref=dst, send_sem=send, recv_sem=recv,
            device_id=device, device_id_type=pl.DeviceIdType.MESH,
        )

    loads = [
        pltpu.make_async_copy(q_hbm, q_buf, in_sem.at[0]),
        pltpu.make_async_copy(qr_hbm, qr_buf, in_sem.at[1]),
        pltpu.make_async_copy(o_hbm, o_buf, in_sem.at[2]),
    ]
    for copy in loads:
        copy.start()

    barrier = pltpu.get_barrier_semaphore()
    greeted = (
        [at(y, x, p) for p in z_peers]
        + [at(y, p, z) for p in x_peers]
        + [at(y_up, x, z), at(y_down, x, z), {"ctx": c_next}, {"ctx": c_prev}, sibling, partner]
    )
    for device in greeted:
        pl.semaphore_signal(barrier, inc=1, device_id=device, device_id_type=pl.DeviceIdType.MESH)

    half = wk_ref.shape[1] // 2
    for q in range(4):
        rows = (wk_ref, wv_ref)[q // 2][...].astype(F32)
        pack[4 * q : 4 * q + 4, :] = rows[:, (q % 2) * half : (q % 2 + 1) * half]
    zbuf[z] = pack[...].astype(BF16)
    lat_win[1] = lat_ref[...]
    rope = rope_ref[...].astype(F32)
    rot_win[1] = jnp.concatenate([rope, rope], axis=1).astype(BF16)

    pl.semaphore_wait(barrier, len(greeted))

    def z_copy(d, slot):
        return remote(zbuf.at[slot], zbuf.at[slot], z_send.at[d], z_recv.at[d], at(y, x, z_peers[d]))

    for d in range(3):
        z_copy(d, z).start()

    halo = [
        remote(lat_win.at[1], lat_win.at[0], h_send.at[0], h_recv.at[0], {"ctx": c_next}),
        remote(lat_win.at[1], lat_win.at[2], h_send.at[1], h_recv.at[1], {"ctx": c_prev}),
        remote(rot_win.at[1], rot_win.at[0], h_send.at[2], h_recv.at[2], {"ctx": c_next}),
        remote(rot_win.at[1], rot_win.at[2], h_send.at[3], h_recv.at[3], {"ctx": c_prev}),
    ]
    for copy in halo:
        copy.start()

    blocks = [lax.rem(me + tokens + b - 1, tokens) for b in range(3)]
    index = lax.broadcasted_iota(jnp.int32, (1, len_ref.shape[1]), 1)
    lengths = len_ref[...]

    def frames(pos, block):
        start = jnp.sum(jnp.where(index <= block, lengths, 0), axis=1, keepdims=True)
        return block + (pos >= start).astype(jnp.int32)

    own = jnp.broadcast_to(pos_ref[pl.ds(me, 1), :], (TOK, TOK))
    own_pos = jnp.transpose(own)
    own_frame = frames(own_pos, me)
    for b in range(3):
        pos = jnp.broadcast_to(pos_ref[pl.ds(blocks[b], 1), :], (TOK, TOK))
        ok = (frames(pos, blocks[b]) <= own_frame) & (own_pos - pos < WINDOW)
        if b == 0:
            ok = ok & jnp.broadcast_to(me > 0, ok.shape)
        if b == 2:
            ok = ok & jnp.broadcast_to(me < tokens - 1, ok.shape)
        bias[:, b * TOK : (b + 1) * TOK] = jnp.where(ok, 0.0, MASKED)
    acc[...] = jnp.zeros_like(acc)

    for d in range(3):
        z_copy(d, z_peers[2 - d]).wait_recv()
    for s in range(NZ):
        piece = zbuf[s].astype(F32)
        for q in range(4):
            mix[q, 4 * s : 4 * s + 4, :] = piece[4 * q : 4 * q + 4, :]
    for j in range(PAIRS):
        lanes = slice((j % 4) * PAIR, (j % 4 + 1) * PAIR)
        wk[j, y, x] = mix[j // 4, :, lanes].astype(BF16)
        wv[j, y, x] = mix[2 + j // 4, :, lanes].astype(BF16)

    up, down = at(y_up, x, z), at(y_down, x, z)
    left, right = at(y, x_down, z), at(y, x_up, z)

    def y_of(steps):
        return lax.rem(y + steps + NY, NY)

    def x_of(steps):
        return lax.rem(x + steps + NX, NX)

    def k_hop(j, sign, depth, offset):
        part = wk.at[j, y_of(offset)]
        if depth == 3:
            part = part.at[0:2] if sign > 0 else part.at[2:4]
        n = 3 + 2 * depth + (0 if sign > 0 else 1)
        return remote(part, part, c_send.at[j, n], c_recv.at[j, n], up if sign > 0 else down)

    def k_x(j, d, offset):
        part = wk.at[j, y, x_of(offset)]
        return remote(part, part, c_send.at[j, d], c_recv.at[j, d], at(y, x_peers[d], z))

    def v_hop(j, sign, depth, offset):
        part = wv.at[j, y_of(offset), x]
        if depth == 3:
            part = part.at[:, 0:DIM] if sign > 0 else part.at[:, DIM:PAIR]
        n = 11 + 2 * depth + (0 if sign > 0 else 1)
        return remote(part, part, c_send.at[j, n], c_recv.at[j, n], up if sign > 0 else down)

    def v_x(j, sign, depth, offset):
        part = wv.at[j, :, x_of(offset)]
        if depth == 1:
            part = wv.at[j, 0:4, x_of(offset)] if sign > 0 else wv.at[j, 4:8, x_of(offset)]
        n = 19 + 2 * depth + (0 if sign > 0 else 1)
        return remote(part, part, c_send.at[j, n], c_recv.at[j, n], right if sign > 0 else left)

    def arrive(make, j, sign, depth):
        make(j, sign, depth, -sign * (depth + 1)).wait_recv()

    def leave(make, j, sign, depth):
        return make(j, sign, depth, -sign * depth)

    def stage(s, j):
        if s == 0:
            for d in range(3):
                k_x(j, d, 0).start()
            for sign in (1, -1):
                leave(v_hop, j, sign, 0).start()
            return
        if s == 1:
            for d in range(3):
                k_x(j, d, -(d + 1)).wait_recv()
            for sign in (1, -1):
                leave(k_hop, j, sign, 0).start()
        elif s <= 5:
            for sign in (1, -1):
                arrive(k_hop, j, sign, s - 2)
                if s <= 4:
                    leave(k_hop, j, sign, s - 1).start()
        if s <= 4:
            for sign in (1, -1):
                arrive(v_hop, j, sign, s - 1)
                if s <= 3:
                    leave(v_hop, j, sign, s).start()
            if s == 4:
                for sign in (1, -1):
                    leave(v_x, j, sign, 0).start()
        elif s == 5:
            for sign in (1, -1):
                arrive(v_x, j, sign, 0)
                leave(v_x, j, sign, 1).start()
        else:
            for sign in (1, -1):
                arrive(v_x, j, sign, 1)

    def outs(j):
        pair = pl.ds(pl.multiple_of(j * PAIR, PAIR), PAIR)
        rot = pl.ds(pl.multiple_of(j * DIM, DIM), DIM)
        return [
            pltpu.make_async_copy(att_buf.at[:, pair], att_hbm.at[:, pair], out_sem.at[j, 0]),
            pltpu.make_async_copy(dq_buf.at[:, pair], dq_hbm.at[:, pair], out_sem.at[j, 1]),
            pltpu.make_async_copy(dqr_buf.at[:, rot], dqr_hbm.at[:, rot], out_sem.at[j, 2]),
        ]

    def compute(j):
        pair = pl.ds(pl.multiple_of(j * PAIR, PAIR), PAIR)
        rot_cols = pl.ds(pl.multiple_of(j * DIM, DIM), DIM)
        window = lat_win[...].reshape(3 * TOK, LATENT)
        rot = rot_win[...].reshape(3 * TOK, 2 * ROPE)
        key_w = wk[j].reshape(LATENT, PAIR)
        value_w = wv[j].reshape(LATENT, PAIR)
        keys = dot(window, key_w, 1, 0).astype(BF16)
        values = dot(window, value_w, 1, 0).astype(BF16)
        q_pair, o_pair, r_pair = q_buf[:, pair], o_buf[:, pair], qr_buf[:, rot_cols]
        first = lax.broadcasted_iota(jnp.int32, (TOK, 2 * ROPE), 1) < ROPE
        blank = jnp.zeros_like(r_pair)
        key_parts, value_parts, attended, grads, rot_grads = [], [], [], [], []
        rot_part = None
        for e in range(2):
            cols = slice(e * DIM, (e + 1) * DIM)
            value, cot = values[:, cols], o_pair[:, cols]
            r_own = jnp.where(first, r_pair, blank) if e == 0 else jnp.where(first, blank, r_pair)
            key_full = jnp.concatenate([keys[:, cols], rot], axis=1)
            query_full = jnp.concatenate([q_pair[:, cols], r_own], axis=1)
            scores = dot(query_full, key_full, 1, 1) * SCALE + bias[...]
            top = jnp.max(scores, axis=1, keepdims=True)
            weights = jnp.exp(scores - top)
            weights = weights * (1.0 / jnp.sum(weights, axis=1, keepdims=True))
            probs = weights.astype(BF16)
            out = dot(probs, value, 1, 0).astype(BF16)
            delta = jnp.sum(cot.astype(F32) * out.astype(F32), axis=1, keepdims=True)
            prob_grad = dot(cot, value, 1, 1)
            score_grad = (weights * (prob_grad - delta)).astype(BF16)
            grad = dot(score_grad, key_full, 1, 0) * SCALE
            key_side = dot(score_grad, query_full, 0, 0) * SCALE
            value_side = dot(probs, cot, 0, 0)
            attended.append(out)
            grads.append(grad[:, :DIM])
            rot_grads.append(grad[:, DIM:])
            key_parts.append(key_side[:, :DIM].astype(BF16))
            value_parts.append(value_side.astype(BF16))
            rot_part = key_side[:, DIM:] if rot_part is None else rot_part + key_side[:, DIM:]
        att_buf[:, pair] = jnp.concatenate(attended, axis=1)
        dq_buf[:, pair] = jnp.concatenate(grads, axis=1)
        dqr_buf[:, rot_cols] = jnp.where(first, rot_grads[0], rot_grads[1])
        back = dot(jnp.concatenate(key_parts, axis=1), key_w, 1, 1)
        back = back + dot(jnp.concatenate(value_parts, axis=1), value_w, 1, 1)
        acc[:, :, :, :LATENT] += back.reshape(3, 2, TOK // 2, LATENT)
        acc[:, :, :, LATENT:] += rot_part.reshape(3, 2, TOK // 2, 2 * ROPE)
        for copy in outs(j):
            copy.start()

    def slot(t, carry):
        for s in reversed(range(STAGES)):
            j = t - LAG * s

            @pl.when((j >= 0) & (j < PAIRS))
            def _(s=s, j=j):
                stage(s, j)

        last = t - LAG * (STAGES - 1)

        @pl.when(last == 0)
        def _():
            for copy in loads:
                copy.wait()
            for copy in halo:
                copy.wait_recv()

        @pl.when(last >= 0)
        def _():
            compute(last)

        return carry

    lax.fori_loop(0, PAIRS + LAG * (STAGES - 1), slot, 0)

    rows = TOK // 2

    def halves(e):
        both = acc[:, e]
        rot = both[:, :, LATENT:].reshape(3 * rows, 2 * ROPE)
        rot = (rot + pltpu.roll(rot, ROPE, 1)).reshape(3, rows, 2 * ROPE)
        return both[:, :, :LATENT], rot

    sent_lat, sent_rot = halves(1 - core)
    t1_src[:, :, :LATENT] = sent_lat.astype(BF16)
    t1_src[:, :, LATENT:] = sent_rot.astype(BF16)
    step1 = remote(t1_src, t1_dst, t_send.at[0], t_recv.at[0], sibling)
    step1.start()
    own_lat, own_rot = halves(core)
    mine[:, :, :LATENT] = own_lat
    mine[:, :, LATENT:] = own_rot
    step1.wait_recv()
    got = t1_dst[...].astype(F32)
    t2_src[0] = (mine[0] + got[0]).astype(BF16)
    t2_src[1] = (mine[2] + got[2]).astype(BF16)
    step2 = [
        remote(t2_src.at[0], t2_dst.at[0], t_send.at[1], t_recv.at[1], {"ctx": c_prev}),
        remote(t2_src.at[1], t2_dst.at[1], t_send.at[2], t_recv.at[2], {"ctx": c_next}),
    ]
    for copy in step2:
        copy.start()
    centre = mine[1] + got[1]
    for copy in step2:
        copy.wait_recv()
    t3_src[...] = (centre + t2_dst[0].astype(F32) + t2_dst[1].astype(F32)).astype(BF16)
    step3 = remote(t3_src, t3_dst, t_send.at[3], t_recv.at[3], partner)
    step3.start()
    step3.wait_recv()
    t4[core] = t3_src[...].astype(F32) + t3_dst[...].astype(F32)
    step4 = remote(t4.at[core], t4.at[core], t_send.at[4], t_recv.at[4], sibling)
    step4.start()
    other = remote(t4.at[1 - core], t4.at[1 - core], t_send.at[4], t_recv.at[4], sibling)
    other.wait_recv()
    whole = t4[...].reshape(TOK, JOINED)
    dlat_ref[...] = whole[:, :LATENT]
    drope_ref[...] = whole[:, LATENT : LATENT + ROPE]

    step1.wait_send()
    for copy in step2:
        copy.wait_send()
    step3.wait_send()
    step4.wait_send()
    for d in range(3):
        z_copy(d, z).wait_send()
    for copy in halo:
        copy.wait_send()

    def drain(j, carry):
        for d in range(3):
            k_x(j, d, 0).wait_send()
        for sign in (1, -1):
            for depth in range(4):
                leave(k_hop, j, sign, depth).wait_send()
                leave(v_hop, j, sign, depth).wait_send()
            for depth in range(2):
                leave(v_x, j, sign, depth).wait_send()
        for copy in outs(j):
            copy.wait()
        return carry

    lax.fori_loop(0, PAIRS, drain, 0)


def on_device(q_nope, q_rope, latent, key_rope, w_key, w_value, stripe, frame_len, out_grad):
    cols = q_nope.shape[1]
    rot_cols = q_rope.shape[1]
    positions = stripe.reshape(-1, TOK)
    lengths = frame_len.reshape(1, -1)
    vmem = pl.BlockSpec(memory_space=pltpu.VMEM)
    hbm = pl.BlockSpec(memory_space=pl.ANY)
    rows = TOK // 2
    copies = 23
    dma = pltpu.SemaphoreType.DMA
    return pl.pallas_call(
        kernel,
        out_shape=(
            jax.ShapeDtypeStruct((TOK, cols), BF16),
            jax.ShapeDtypeStruct((TOK, cols), F32),
            jax.ShapeDtypeStruct((TOK, rot_cols), F32),
            jax.ShapeDtypeStruct((TOK, LATENT), F32),
            jax.ShapeDtypeStruct((TOK, ROPE), F32),
        ),
        in_specs=[hbm, hbm, vmem, vmem, vmem, vmem, vmem, vmem, hbm],
        out_specs=(hbm, hbm, hbm, vmem, vmem),
        scratch_shapes=[
            pltpu.VMEM((TOK, cols), BF16),
            pltpu.VMEM((TOK, rot_cols), BF16),
            pltpu.VMEM((TOK, cols), BF16),
            pltpu.VMEM((TOK, cols), BF16),
            pltpu.VMEM((TOK, cols), F32),
            pltpu.VMEM((TOK, rot_cols), F32),
            pltpu.VMEM((16, cols // 2), F32),
            pltpu.VMEM((NZ, 16, cols // 2), BF16),
            pltpu.VMEM((4, 16, cols // 2), F32),
            pltpu.VMEM((PAIRS, NY, NX, 16, PAIR), BF16),
            pltpu.VMEM((PAIRS, NY, NX, 16, PAIR), BF16),
            pltpu.VMEM((3, TOK, LATENT), BF16),
            pltpu.VMEM((3, TOK, 2 * ROPE), BF16),
            pltpu.VMEM((TOK, 3 * TOK), F32),
            pltpu.VMEM((3, 2, rows, JOINED), F32),
            pltpu.VMEM((3, rows, JOINED), BF16),
            pltpu.VMEM((3, rows, JOINED), BF16),
            pltpu.VMEM((2, rows, JOINED), BF16),
            pltpu.VMEM((2, rows, JOINED), BF16),
            pltpu.VMEM((rows, JOINED), BF16),
            pltpu.VMEM((rows, JOINED), BF16),
            pltpu.VMEM((2, rows, JOINED), F32),
            pltpu.VMEM((3, rows, JOINED), F32),
            dma((3,)),
            dma((PAIRS, 3)),
            dma((3,)),
            dma((3,)),
            dma((4,)),
            dma((4,)),
            dma((PAIRS, copies)),
            dma((PAIRS, copies)),
            dma((5,)),
            dma((5,)),
        ],
        compiler_params=pltpu.CompilerParams(
            collective_id=0, has_side_effects=True, vmem_limit_bytes=48 * 1024 * 1024
        ),
        cost_estimate=pl.CostEstimate(flops=4_700_000_000, bytes_accessed=5_000_000, transcendentals=800_000),
        name="latent_attention",
    )(q_nope, q_rope, latent, key_rope, w_key, w_value, positions, lengths, out_grad)


def solution(mesh):
    return jax.shard_map(
        on_device,
        mesh=mesh,
        in_specs=(
            P("ctx", "head"),
            P("ctx", "head"),
            P("ctx", None),
            P("ctx", None),
            P("ctx", "head"),
            P("ctx", "head"),
            P(),
            P(),
            P("ctx", "head"),
        ),
        out_specs=(
            P("ctx", "head"),
            P("ctx", "head"),
            P("ctx", "head"),
            P("ctx", None),
            P("ctx", None),
        ),
        check_vma=False,
    )
```

time: 1510 us -> 100 us (0.07)
  waiting for transfers between devices: 1320 us -> 0 us
  blocking collectives: 107 us -> 0 us
  Pallas kernels: 0 us -> 89.4 us
  matrix products: 24.3 us -> 0 us
    all_gather x2 -> x0, waiting for transfers between devices: 1270 us -> none  [the longest x1 677 us: on_device(): lax.all_gather(w_key, 'ctx', axis=0, tiled=True)]
    psum x1 -> x0, blocking collectives: 107 us -> none  [on_device(): d_latent, d_key_rope = lax.psum((lat_own, rot_own), 'head')]
    pallas_call x0 -> x1, Pallas kernels: none -> 89.4 us  [on_device(): pl.pallas_call(kernel, out_shape=(jax.ShapeDtypeStruct((TOK, cols), BF16)...]
    psum x1 -> x0, waiting for transfers between devices: 43.7 us -> none  [on_device(): d_latent, d_key_rope = lax.psum((lat_own, rot_own), 'head')]
    dot_general x13 -> x0, matrix products: 24.3 us -> none  [the longest x1 3.79 us: on_device(): keys_now = jnp.dot(source, key_weight, preferred_element_type=jnp.float32)]
  transfers between devices with their start and end apart: 7 -> 0, of which waited for: 4 -> 0; matrix products, arithmetic and copies ran while one was open for 2% -> 0% of each run, Pallas kernels for 0% -> 0%
where the time goes in v1:
time: 100 us; the launch traced here: 99.7 us
  Pallas kernels  89.4 us (89%)
  local copies, waits for them, and re-layouts  9.58 us (10%)
    pallas_call x1, Pallas kernels, on_device(): pl.pallas_call(kernel, out_shape=(jax.ShapeDtypeStruct((TOK, cols), BF16)...  89.4 us
    unnamed x21, local copies, waits for them, and re-layouts  8.88 us

profile of v1, /device:TPU:1, one launch (start us, length us, event | category | flops | bytes accessed | tf_op | source)
XLA Modules:
  0.0 99.7 jit_solution(11787624144412602720)
XLA Ops:
  0.6 0.0 copy-start.5
  0.6 0.0 copy-start.6
  0.7 0.0 copy-start.7
  0.7 0.8 copy.14.rope_ref
  1.5 0.0 copy-done.5
  1.5 0.0 copy-done.6
  1.5 0.0 copy-done.7
  1.5 0.0 copy-start
  1.5 1.0 %copy-done = bf16[128,2048]{1,0:T(8,128)(2,1)S(1)} copy-done((bf16[128,2048]{1,0:T(8,128)(2,1)S(1)}, bf16[128,2048]{1,0:T(8,128)(2,1)}, u32[]{:S(2)}) %copy-start) | copy-done | bytes 524312
  2.6 0.0 copy-start.1
  2.6 1.0 %copy-done.1 = bf16[128,2048]{1,0:T(8,128)(2,1)S(1)} copy-done((bf16[128,2048]{1,0:T(8,128)(2,1)S(1)}, bf16[128,2048]{1,0:T(8,128)(2,1)}, u32[]{:S(2)}) %copy-start.1) | copy-done | bytes 524312
  3.6 0.0 copy-start.2
  3.6 0.9 copy-done.2
  4.6 0.0 copy-start.3
  4.6 0.9 copy-done.3
  5.5 0.0 copy-start.4
  5.5 0.8 copy-done.4
  6.3 89.4 %latent_attention.1 = (bf16[128,2048]{1,0:T(8,128)(2,1)S(1)}, f32[128,2048]{1,0:T(8,128)S(1)}, f32[128,1024]{1,0:T(8,128)S(1)}, f32[128,512]{1,0:T(8,128)S(1)}, f32[128,64]{1,0:T(8,128)S(1)}) custom-call(bf16[128,2048]{1,0:T(8,128)(2,1)S(1)} %copy-done, bf16[128,1024]{1,0:T(8,128)(2,1)S(1)} %copy-done.2, bf16[128,512]{1,0:T(8,128)(2,1)S(1)} %copy-done.3, ...), custom_call_target="tpu_custom_call" | custom-call | flops 4700000256 | bytes 5000000 | tf_op jit(solution)/shard_map/latent_attention/pallas_call | solution.py:374
  95.8 0.7 copy.15
  96.5 0.8 copy.20
  97.2 1.0 copy.21
  98.2 0.8 copy.22
  99.0 0.7 copy.23
Async XLA Ops:
  0.6 0.9 copy-start.5
  0.6 0.9 copy-start.6
  0.7 0.9 copy-start.7
  1.5 1.0 %copy-start = (bf16[128,2048]{1,0:T(8,128)(2,1)S(1)}, bf16[128,2048]{1,0:T(8,128)(2,1)}, u32[]{:S(2)}) copy-start(bf16[128,2048]{1,0:T(8,128)(2,1)} %q_hbm.1) | copy-start | bytes 1572868
  2.6 1.0 %copy-start.1 = (bf16[128,2048]{1,0:T(8,128)(2,1)S(1)}, bf16[128,2048]{1,0:T(8,128)(2,1)}, u32[]{:S(2)}) copy-start(bf16[128,2048]{1,0:T(8,128)(2,1)} %o_hbm.1) | copy-start | bytes 1572868
  3.6 0.9 copy-start.2
  4.6 0.9 copy-start.3
  5.5 0.8 copy-start.4

commit v2 on v1

v2 whole, which is shorter than its diff:
```python
import jax
import jax.numpy as jnp
from jax import lax
from jax.experimental import pallas as pl
from jax.experimental.pallas import tpu as pltpu
from jax.sharding import PartitionSpec as P

HEAD_QK = 192
WINDOW = 128
SCALE = HEAD_QK ** (-0.5)
MASKED = -1e30
VMEM_BYTES = 60 * 1024 * 1024

NY, NX, NZ = 8, 4, 4
TOK = 128
LATENT = 512
ROPE = 64
DIM = 128
CHUNKS = 4
WIDTH = 4 * DIM
ROWS = LATENT + ROPE
HALF = ROWS // 2
K_SLOTS = (0, 1, 2, 3, 4)
V_SLOTS = (2, 3, 4)
K_GROUPS = ((0, 1), (1, CHUNKS))
V_GROUP = (1, CHUNKS)

BF16 = jnp.bfloat16
F32 = jnp.float32


def dot(a, b, ca, cb):
    return lax.dot_general(a, b, (((ca,), (cb,)), ((), ())), preferred_element_type=F32)


def kernel(
    q_hbm, qr_hbm, lat_hbm, rope_hbm, wk_ref, wv_ref, pos_hbm, len_ref, o_hbm,
    att_hbm, dq_hbm, dqr_hbm, dlat_ref, drope_ref,
    q_buf, qr_buf, o_buf, rope_buf, pos_ref, att_buf, dq_buf, dqr_buf,
    pack, zbuf, mix, wk, wv, lat_win, rot_win, bias, acc,
    t1_src, t1_dst, t2_src, t2_dst, t3_src, t3_dst, t4,
    in_sem, out_sem, z_send, z_recv, h_send, h_recv, g_send, g_recv, c_send, c_recv, t_send, t_recv,
):
    me = lax.axis_index("ctx")
    head = lax.axis_index("head")
    z = lax.rem(me, NZ)
    x = lax.rem(lax.div(me, NZ), NX)
    y = lax.div(me, NZ * NX)
    core = lax.rem(head, 2)
    z_hi = lax.div(head, 2)

    def at(y_, x_, z_):
        return {"ctx": (y_ * NX + x_) * NZ + z_}

    z_peers = [lax.rem(z + d, NZ) for d in (1, 2, 3)]
    x_peers = [lax.rem(x + d, NX) for d in (1, 2, 3)]
    y_peers = [lax.rem(y + d, NY) for d in range(1, NY)]
    y_up, y_down = y_peers[0], y_peers[-1]
    x_up, x_down = x_peers[0], x_peers[2]
    tokens = NY * NX * NZ
    c_next, c_prev = lax.rem(me + 1, tokens), lax.rem(me + tokens - 1, tokens)
    sibling = {"head": z_hi * 2 + (1 - core)}
    partner = {"head": (1 - z_hi) * 2 + core}

    def remote(src, dst, send, recv, device):
        return pltpu.make_async_remote_copy(
            src_ref=src, dst_ref=dst, send_sem=send, recv_sem=recv,
            device_id=device, device_id_type=pl.DeviceIdType.MESH,
        )

    loads = [
        pltpu.make_async_copy(q_hbm, q_buf, in_sem.at[0]),
        pltpu.make_async_copy(qr_hbm, qr_buf, in_sem.at[1]),
        pltpu.make_async_copy(o_hbm, o_buf, in_sem.at[2]),
    ]
    early = [
        pltpu.make_async_copy(lat_hbm, lat_win.at[1], in_sem.at[3]),
        pltpu.make_async_copy(rope_hbm, rope_buf, in_sem.at[4]),
        pltpu.make_async_copy(pos_hbm, pos_ref, in_sem.at[5]),
    ]
    for copy in early + loads:
        copy.start()

    barrier = pltpu.get_barrier_semaphore()
    greeted = (
        [at(y, x, p) for p in z_peers]
        + [at(y, p, z) for p in x_peers]
        + [at(p, x, z) for p in y_peers]
        + [{"ctx": c_next}, {"ctx": c_prev}, sibling, partner]
    )
    for device in greeted:
        pl.semaphore_signal(barrier, inc=1, device_id=device, device_id_type=pl.DeviceIdType.MESH)

    half = wk_ref.shape[1] // 2
    for q in range(4):
        rows = (wk_ref, wv_ref)[q // 2][...].astype(F32)
        pack[4 * q : 4 * q + 4, :] = rows[:, (q % 2) * half : (q % 2 + 1) * half]
    zbuf[z] = pack[...].astype(BF16)
    for copy in early:
        copy.wait()
    rope = jnp.transpose(rope_buf[...].astype(F32))
    rot_win[1] = jnp.concatenate([rope, rope], axis=1).astype(BF16)

    pl.semaphore_wait(barrier, len(greeted))

    def z_copy(d, slot):
        return remote(zbuf.at[slot], zbuf.at[slot], z_send.at[d], z_recv.at[d], at(y, x, z_peers[d]))

    for d in range(3):
        z_copy(d, z).start()

    blocks = [lax.rem(me + tokens + b - 1, tokens) for b in range(3)]
    index = lax.broadcasted_iota(jnp.int32, (1, len_ref.shape[1]), 1)
    lengths = len_ref[...]

    def frames(pos, block):
        start = jnp.sum(jnp.where(index <= block, lengths, 0), axis=1, keepdims=True)
        return block + (pos >= start).astype(jnp.int32)

    own = jnp.broadcast_to(pos_ref[pl.ds(me, 1), :], (TOK, TOK))
    own_pos = jnp.transpose(own)
    own_frame = frames(own_pos, me)
    for b in range(3):
        pos = jnp.broadcast_to(pos_ref[pl.ds(blocks[b], 1), :], (TOK, TOK))
        ok = (frames(pos, blocks[b]) <= own_frame) & (own_pos - pos < WINDOW)
        if b == 0:
            ok = ok & jnp.broadcast_to(me > 0, ok.shape)
        if b == 2:
            ok = ok & jnp.broadcast_to(me < tokens - 1, ok.shape)
        bias[:, b * TOK : (b + 1) * TOK] = jnp.where(ok, 0.0, MASKED)
    acc[...] = jnp.zeros_like(acc)

    for d in range(3):
        z_copy(d, z_peers[2 - d]).wait_recv()
    for s in range(NZ):
        piece = zbuf[s].astype(F32)
        for q in range(4):
            mix[q, 4 * s : 4 * s + 4, :] = piece[4 * q : 4 * q + 4, :]
    for j in range(CHUNKS):
        lanes = slice((j % 2) * WIDTH, (j % 2 + 1) * WIDTH)
        wk[j, y, x] = mix[j // 2, :, lanes].astype(BF16)
        wv[j, y, x] = mix[2 + j // 2, :, lanes].astype(BF16)

    up, down = at(y_up, x, z), at(y_down, x, z)
    left, right = at(y, x_down, z), at(y, x_up, z)

    def y_of(steps):
        return lax.rem(y + steps + NY, NY)

    def x_of(steps):
        return lax.rem(x + steps + NX, NX)

    def k_x(g, d, offset):
        part = wk.at[slice(*K_GROUPS[g]), y, x_of(offset)]
        n = 3 * g + d
        return remote(part, part, g_send.at[n], g_recv.at[n], at(y, x_peers[d], z))

    def v_direct(d, offset):
        part = wv.at[0, y_of(offset), x]
        n = 6 + d
        return remote(part, part, g_send.at[n], g_recv.at[n], at(y_peers[d], x, z))

    def v_hop(_, sign, depth, offset):
        part = wv.at[slice(*V_GROUP), y_of(offset), x]
        if depth == 3:
            part = part.at[:, :, : WIDTH // 2] if sign > 0 else part.at[:, :, WIDTH // 2 :]
        n = 13 + 2 * depth + (0 if sign > 0 else 1)
        return remote(part, part, g_send.at[n], g_recv.at[n], up if sign > 0 else down)

    def k_hop(j, sign, depth, offset):
        part = wk.at[j, y_of(offset)]
        if depth == 3:
            part = part.at[0:2] if sign > 0 else part.at[2:4]
        n = 2 * depth + (0 if sign > 0 else 1)
        return remote(part, part, c_send.at[j, n], c_recv.at[j, n], up if sign > 0 else down)

    def v_x(j, sign, depth, offset):
        part = wv.at[j, :, x_of(offset)]
        if depth == 1:
            part = wv.at[j, 0:4, x_of(offset)] if sign > 0 else wv.at[j, 4:8, x_of(offset)]
        n = 8 + 2 * depth + (0 if sign > 0 else 1)
        return remote(part, part, c_send.at[j, n], c_recv.at[j, n], right if sign > 0 else left)

    def arrive(make, j, sign, depth):
        make(j, sign, depth, -sign * (depth + 1)).wait_recv()

    def leave(make, j, sign, depth):
        return make(j, sign, depth, -sign * depth)

    def hop(make, j, n, last):
        for sign in (1, -1):
            if n > 0:
                arrive(make, j, sign, n - 1)
            if n < last:
                leave(make, j, sign, n).start()

    for d in range(NY - 1):
        v_direct(d, 0).start()
    for g in range(2):
        for d in range(3):
            k_x(g, d, 0).start()
        if g == 0:
            hop(v_hop, 0, 0, 4)

    halo = [
        remote(lat_win.at[1], lat_win.at[0], h_send.at[0], h_recv.at[0], {"ctx": c_next}),
        remote(lat_win.at[1], lat_win.at[2], h_send.at[1], h_recv.at[1], {"ctx": c_prev}),
        remote(rot_win.at[1], rot_win.at[0], h_send.at[2], h_recv.at[2], {"ctx": c_next}),
        remote(rot_win.at[1], rot_win.at[2], h_send.at[3], h_recv.at[3], {"ctx": c_prev}),
    ]
    for copy in halo:
        copy.start()

    def columns(j, width):
        return pl.ds(pl.multiple_of(j * width, width), width)

    def outs(j):
        plain, rot = columns(j, WIDTH), columns(j, WIDTH // 2)
        return [
            pltpu.make_async_copy(att_buf.at[:, plain], att_hbm.at[:, plain], out_sem.at[j, 0]),
            pltpu.make_async_copy(dq_buf.at[:, plain], dq_hbm.at[:, plain], out_sem.at[j, 1]),
            pltpu.make_async_copy(dqr_buf.at[:, rot], dqr_hbm.at[:, rot], out_sem.at[j, 2]),
        ]

    def compute(j):
        plain, rot_cols = columns(j, WIDTH), columns(j, WIDTH // 2)
        window = lat_win[...].reshape(3 * TOK, LATENT)
        rot = rot_win[...].reshape(3 * TOK, 2 * ROPE)
        key_w = wk[j].reshape(LATENT, WIDTH)
        value_w = wv[j].reshape(LATENT, WIDTH)
        keys = dot(window, key_w, 1, 0).astype(BF16)
        values = dot(window, value_w, 1, 0).astype(BF16)
        queries, cots, rots = q_buf[:, plain], o_buf[:, plain], qr_buf[:, rot_cols]
        first = lax.broadcasted_iota(jnp.int32, (TOK, 2 * ROPE), 1) < ROPE
        blank = jnp.zeros((TOK, 2 * ROPE), BF16)
        key_parts, value_parts, attended, grads, rot_grads = [], [], [], [], []
        rot_part = None
        for e in range(4):
            cols = slice(e * DIM, (e + 1) * DIM)
            value, cot = values[:, cols], cots[:, cols]
            r_pair = rots[:, (e // 2) * DIM : (e // 2 + 1) * DIM]
            r_own = jnp.where(first, r_pair, blank) if e % 2 == 0 else jnp.where(first, blank, r_pair)
            key_full = jnp.concatenate([keys[:, cols], rot], axis=1)
            query_full = jnp.concatenate([queries[:, cols], r_own], axis=1)
            scores = dot(query_full, key_full, 1, 1) * SCALE + bias[...]
            top = jnp.max(scores, axis=1, keepdims=True)
            weights = jnp.exp(scores - top)
            weights = weights * (1.0 / jnp.sum(weights, axis=1, keepdims=True))
            probs = weights.astype(BF16)
            out = dot(probs, value, 1, 0).astype(BF16)
            delta = jnp.sum(cot.astype(F32) * out.astype(F32), axis=1, keepdims=True)
            prob_grad = dot(cot, value, 1, 1)
            score_grad = (weights * (prob_grad - delta)).astype(BF16)
            grad = dot(score_grad, key_full, 1, 0) * SCALE
            key_side = dot(query_full, score_grad, 0, 0) * SCALE
            value_parts.append(dot(cot, probs, 0, 0).astype(BF16))
            key_parts.append(key_side[:DIM].astype(BF16))
            rot_part = key_side[DIM:] if rot_part is None else rot_part + key_side[DIM:]
            attended.append(out)
            grads.append(grad[:, :DIM])
            rot_grads.append(grad[:, DIM:])
        att_buf[:, plain] = jnp.concatenate(attended, axis=1)
        dq_buf[:, plain] = jnp.concatenate(grads, axis=1)
        dqr_buf[:, rot_cols] = jnp.concatenate(
            [jnp.where(first, rot_grads[e], rot_grads[e + 1]) for e in (0, 2)], axis=1
        )
        back = dot(key_w, jnp.concatenate(key_parts, axis=0), 1, 0)
        acc[:LATENT] += back + dot(value_w, jnp.concatenate(value_parts, axis=0), 1, 0)
        acc[LATENT:] += rot_part
        for copy in outs(j):
            copy.start()

    def slot(t, carry):
        def during(j, run):
            @pl.when((j >= 0) & (j < CHUNKS))
            def _():
                run(j)

        def once(when, run):
            @pl.when(t == when)
            def _():
                run()

        def k_arrive(g):
            for d in range(3):
                k_x(g, d, -(d + 1)).wait_recv()

        def v_arrive():
            for d in range(NY - 1):
                v_direct(d, -(d + 1)).wait_recv()

        for n in reversed(range(1, 5)):
            during(t - K_SLOTS[n], lambda j, n=n: hop(k_hop, j, n, 4))
        for n in reversed(range(1, 3)):
            during(t - V_SLOTS[n], lambda j, n=n: hop(v_x, j, n, 2))
        for g in range(2):
            once(g, lambda g=g: k_arrive(g))
        during(t - K_SLOTS[0], lambda j: hop(k_hop, j, 0, 4))
        once(V_SLOTS[0], v_arrive)
        for n in range(1, 5):
            once(n - 1, lambda n=n: hop(v_hop, 0, n, 4))
        during(t - V_SLOTS[0], lambda j: hop(v_x, j, 0, 2))

        last = t - max(K_SLOTS[-1], V_SLOTS[-1])

        @pl.when(last == 0)
        def _():
            for copy in loads:
                copy.wait()
            for copy in halo:
                copy.wait_recv()

        @pl.when(last >= 0)
        def _():
            compute(last)

        return carry

    lax.fori_loop(0, CHUNKS + max(K_SLOTS[-1], V_SLOTS[-1]), slot, 0)

    acc[LATENT:ROWS] += acc[ROWS:]
    t1_src[...] = acc[pl.ds(pl.multiple_of((1 - core) * HALF, HALF), HALF)].astype(BF16)
    step1 = remote(t1_src, t1_dst, t_send.at[0], t_recv.at[0], sibling)
    step1.start()
    mine = acc[pl.ds(pl.multiple_of(core * HALF, HALF), HALF)]
    step1.wait_recv()
    mine = mine + t1_dst[...].astype(F32)
    t2_src[0] = mine[:, :TOK].astype(BF16)
    t2_src[1] = mine[:, 2 * TOK :].astype(BF16)
    step2 = [
        remote(t2_src.at[0], t2_dst.at[0], t_send.at[1], t_recv.at[1], {"ctx": c_prev}),
        remote(t2_src.at[1], t2_dst.at[1], t_send.at[2], t_recv.at[2], {"ctx": c_next}),
    ]
    for copy in step2:
        copy.start()
    for copy in step2:
        copy.wait_recv()
    t3_src[...] = (mine[:, TOK : 2 * TOK] + t2_dst[0].astype(F32) + t2_dst[1].astype(F32)).astype(BF16)
    step3 = remote(t3_src, t3_dst, t_send.at[3], t_recv.at[3], partner)
    step3.start()
    step3.wait_recv()
    t4[core] = t3_src[...].astype(F32) + t3_dst[...].astype(F32)
    step4 = remote(t4.at[core], t4.at[core], t_send.at[4], t_recv.at[4], sibling)
    step4.start()
    other = remote(t4.at[1 - core], t4.at[1 - core], t_send.at[4], t_recv.at[4], sibling)
    other.wait_recv()
    whole = t4[...].reshape(ROWS, TOK)
    dlat_ref[...] = jnp.transpose(whole[:LATENT])
    drope_ref[...] = whole[LATENT:]

    step1.wait_send()
    for copy in step2:
        copy.wait_send()
    step3.wait_send()
    step4.wait_send()
    for d in range(3):
        z_copy(d, z).wait_send()
    for copy in halo:
        copy.wait_send()

    for d in range(NY - 1):
        v_direct(d, 0).wait_send()
    for d in range(3):
        k_x(0, d, 0).wait_send()
        k_x(1, d, 0).wait_send()
    for sign in (1, -1):
        for depth in range(4):
            leave(v_hop, 0, sign, depth).wait_send()

    def drain(j, carry):
        for sign in (1, -1):
            for depth in range(4):
                leave(k_hop, j, sign, depth).wait_send()
            for depth in range(2):
                leave(v_x, j, sign, depth).wait_send()
        for copy in outs(j):
            copy.wait()
        return carry

    lax.fori_loop(0, CHUNKS, drain, 0)


PARTS = (1, 2, 1, 1, 1)


def write_out(*refs):
    count = len(PARTS)
    sources, targets, buffers = refs[:count], refs[count : 2 * count], refs[2 * count : 3 * count]
    came, left = refs[3 * count :]
    moves = []
    for source, target, buffer, parts in zip(sources, targets, buffers, PARTS):
        size = source.shape[0] // parts
        for p in range(parts):
            n = len(moves)
            rows = slice(p * size, (p + 1) * size)
            moves.append((
                pltpu.make_async_copy(source.at[rows], buffer.at[rows], came.at[n]),
                pltpu.make_async_copy(buffer.at[rows], target.at[rows], left.at[n]),
            ))
    for load, _ in moves:
        load.start()
    for load, store in moves:
        load.wait()
        store.start()
    for _, store in moves:
        store.wait()


def on_device(q_nope, q_rope, latent, key_rope, w_key, w_value, stripe, frame_len, out_grad):
    cols = q_nope.shape[1]
    rot_cols = q_rope.shape[1]
    positions = stripe.reshape(-1, TOK)
    lengths = frame_len.reshape(1, -1)
    vmem = pl.BlockSpec(memory_space=pltpu.VMEM)
    hbm = pl.BlockSpec(memory_space=pltpu.HBM)
    dma = pltpu.SemaphoreType.DMA
    outs = (
        jax.ShapeDtypeStruct((TOK, cols), BF16),
        jax.ShapeDtypeStruct((TOK, cols), F32),
        jax.ShapeDtypeStruct((TOK, rot_cols), F32),
        jax.ShapeDtypeStruct((TOK, LATENT), F32),
        jax.ShapeDtypeStruct((ROPE, TOK), F32),
    )
    results = pl.pallas_call(
        kernel,
        out_shape=outs,
        in_specs=[hbm, hbm, hbm, hbm, vmem, vmem, hbm, vmem, hbm],
        out_specs=(hbm, hbm, hbm, vmem, vmem),
        scratch_shapes=[
            pltpu.VMEM((TOK, cols), BF16),
            pltpu.VMEM((TOK, rot_cols), BF16),
            pltpu.VMEM((TOK, cols), BF16),
            pltpu.VMEM((ROPE, TOK), BF16),
            pltpu.VMEM(positions.shape, jnp.int32),
            pltpu.VMEM((TOK, cols), BF16),
            pltpu.VMEM((TOK, cols), F32),
            pltpu.VMEM((TOK, rot_cols), F32),
            pltpu.VMEM((16, cols // 2), F32),
            pltpu.VMEM((NZ, 16, cols // 2), BF16),
            pltpu.VMEM((4, 16, cols // 2), F32),
            pltpu.VMEM((CHUNKS, NY, NX, 16, WIDTH), BF16),
            pltpu.VMEM((CHUNKS, NY, NX, 16, WIDTH), BF16),
            pltpu.VMEM((3, TOK, LATENT), BF16),
            pltpu.VMEM((3, TOK, 2 * ROPE), BF16),
            pltpu.VMEM((TOK, 3 * TOK), F32),
            pltpu.VMEM((LATENT + 2 * ROPE, 3 * TOK), F32),
            pltpu.VMEM((HALF, 3 * TOK), BF16),
            pltpu.VMEM((HALF, 3 * TOK), BF16),
            pltpu.VMEM((2, HALF, TOK), BF16),
            pltpu.VMEM((2, HALF, TOK), BF16),
            pltpu.VMEM((HALF, TOK), BF16),
            pltpu.VMEM((HALF, TOK), BF16),
            pltpu.VMEM((2, HALF, TOK), F32),
            dma((6,)),
            dma((CHUNKS, 3)),
            dma((3,)),
            dma((3,)),
            dma((4,)),
            dma((4,)),
            dma((21,)),
            dma((21,)),
            dma((CHUNKS, 12)),
            dma((CHUNKS, 12)),
            dma((5,)),
            dma((5,)),
        ],
        compiler_params=pltpu.CompilerParams(
            collective_id=0, has_side_effects=True, vmem_limit_bytes=VMEM_BYTES
        ),
        cost_estimate=pl.CostEstimate(flops=4_700_000_000, bytes_accessed=5_000_000, transcendentals=800_000),
        name="latent_attention",
    )(q_nope, q_rope, latent, key_rope.T, w_key, w_value, positions, lengths, out_grad)
    attended, dq_nope, dq_rope, d_latent, d_key_rope = pl.pallas_call(
        write_out,
        out_shape=outs,
        in_specs=[hbm] * len(outs),
        out_specs=(hbm,) * len(outs),
        compiler_params=pltpu.CompilerParams(vmem_limit_bytes=VMEM_BYTES),
        scratch_shapes=[pltpu.VMEM(out.shape, out.dtype) for out in outs] + [dma((sum(PARTS),))] * 2,
        name="write_out",
    )(*results)
    return attended, dq_nope, dq_rope, d_latent, d_key_rope.T


def solution(mesh):
    return jax.shard_map(
        on_device,
        mesh=mesh,
        in_specs=(
            P("ctx", "head"),
            P("ctx", "head"),
            P("ctx", None),
            P("ctx", None),
            P("ctx", "head"),
            P("ctx", "head"),
            P(),
            P(),
            P("ctx", "head"),
        ),
        out_specs=(
            P("ctx", "head"),
            P("ctx", "head"),
            P("ctx", "head"),
            P("ctx", None),
            P("ctx", None),
        ),
        check_vma=False,
    )
```

time: 100 us -> 88.4 us (0.88)
  local copies, waits for them, and re-layouts: 9.58 us -> 0 us
  Pallas kernels: 89.4 us -> 87.4 us
    unnamed x21 -> x0, local copies, waits for them, and re-layouts: 8.88 us -> none
    pallas_call x1 -> x2, Pallas kernels: 89.4 us -> 87.4 us  [the longest x1 84.9 us: on_device(): pl.pallas_call(kernel, out_shape=outs, in_specs=[hbm, hbm, hbm, hbm, vmem...]
where the time goes in v2:
time: 88.4 us; the launch traced here: 88 us
  Pallas kernels  87.4 us (99%)
    pallas_call x1, Pallas kernels, on_device(): pl.pallas_call(kernel, out_shape=outs, in_specs=[hbm, hbm, hbm, hbm, vmem...  84.9 us
    pallas_call x1, Pallas kernels, on_device(): pl.pallas_call(write_out, out_shape=outs, in_specs=[hbm] * len(outs), out...  2.54 us

profile of v2, /device:TPU:1, one launch (start us, length us, event | category | flops | bytes accessed | tf_op | source)
XLA Modules:
  0.0 88.0 jit_solution(5973010207990578098)
XLA Ops:
  0.6 84.9 %latent_attention.1 = (bf16[128,2048]{1,0:T(8,128)(2,1)}, f32[128,2048]{1,0:T(8,128)}, f32[128,1024]{1,0:T(8,128)}, f32[128,512]{1,0:T(8,128)}, f32[64,128]{1,0:T(8,128)}) custom-call(bf16[128,2048]{1,0:T(8,128)(2,1)} %q_hbm.1, bf16[128,1024]{1,0:T(8,128)(2,1)} %qr_hbm.1, bf16[128,512]{1,0:T(8,128)(2,1)} %lat_hbm.1, bf16[64,128]{1,0:T(8,128)(2,1)} %bitcast.6, ...), custom_call_target="tpu_custom_call" | custom-call | flops 4700000256 | bytes 5000000 | tf_op jit(solution)/shard_map/latent_attention/pallas_call | solution.py:424
  85.5 2.5 %write_out.1 = (bf16[128,2048]{1,0:T(8,128)(2,1)}, f32[128,2048]{1,0:T(8,128)}, f32[128,1024]{1,0:T(8,128)}, f32[128,512]{1,0:T(8,128)}, f32[64,128]{1,0:T(8,128)}) custom-call(bf16[128,2048]{1,0:T(8,128)(2,1)} %get-tuple-element.15.refs_0_, f32[128,2048]{1,0:T(8,128)} %get-tuple-element.16.refs_1_, f32[128,1024]{1,0:T(8,128)} %get-tuple-element.17.refs_2_, ...), custom_call_target="tpu_custom_call" | custom-call | tf_op jit(solution)/shard_map/write_out/pallas_call | solution.py:473

commit v3 on v2

--- a/solution.py
+++ b/solution.py
@@ -16,14 +16,21 @@
 LATENT = 512
 ROPE = 64
 DIM = 128
-CHUNKS = 4
-WIDTH = 4 * DIM
+CHUNKS = 8
+WIDTH = 2 * DIM
+STEPS = CHUNKS // 2
+HEADS = 4
+PIECES = 2
 ROWS = LATENT + ROPE
 HALF = ROWS // 2
-K_SLOTS = (0, 1, 2, 3, 4)
-V_SLOTS = (2, 3, 4)
+PIECE = HALF // PIECES
+K_SLOTS = (0, 3, 5, 7, 9)
+V_SLOTS = (4, 6, 9)
 K_GROUPS = ((0, 1), (1, CHUNKS))
-V_GROUP = (1, CHUNKS)
+DIRECT = 2
+V_GROUP = (DIRECT, CHUNKS)
+V_HOPS = (0, 2, 4, 6)
+LAST = max(K_SLOTS[-1], V_SLOTS[-1])
 
 BF16 = jnp.bfloat16
 F32 = jnp.float32
@@ -34,9 +41,9 @@
 
 
 def kernel(
-    q_hbm, qr_hbm, lat_hbm, rope_hbm, wk_ref, wv_ref, pos_hbm, len_ref, o_hbm,
+    q_hbm, qr_hbm, lat_hbm, rope_hbm, wk_hbm, wv_hbm, pos_hbm, len_hbm, o_hbm,
     att_hbm, dq_hbm, dqr_hbm, dlat_ref, drope_ref,
-    q_buf, qr_buf, o_buf, rope_buf, pos_ref, att_buf, dq_buf, dqr_buf,
+    q_buf, qr_buf, o_buf, rope_buf, pos_ref, wk_ref, wv_ref, len_ref, att_buf, dq_buf, dqr_buf,
     pack, zbuf, mix, wk, wv, lat_win, rot_win, bias, acc,
     t1_src, t1_dst, t2_src, t2_dst, t3_src, t3_dst, t4,
     in_sem, out_sem, z_send, z_recv, h_send, h_recv, g_send, g_recv, c_send, c_recv, t_send, t_recv,
@@ -68,19 +75,6 @@
             device_id=device, device_id_type=pl.DeviceIdType.MESH,
         )
 
-    loads = [
-        pltpu.make_async_copy(q_hbm, q_buf, in_sem.at[0]),
-        pltpu.make_async_copy(qr_hbm, qr_buf, in_sem.at[1]),
-        pltpu.make_async_copy(o_hbm, o_buf, in_sem.at[2]),
-    ]
-    early = [
-        pltpu.make_async_copy(lat_hbm, lat_win.at[1], in_sem.at[3]),
-        pltpu.make_async_copy(rope_hbm, rope_buf, in_sem.at[4]),
-        pltpu.make_async_copy(pos_hbm, pos_ref, in_sem.at[5]),
-    ]
-    for copy in early + loads:
-        copy.start()
-
     barrier = pltpu.get_barrier_semaphore()
     greeted = (
         [at(y, x, p) for p in z_peers]
@@ -91,23 +85,43 @@
     for device in greeted:
         pl.semaphore_signal(barrier, inc=1, device_id=device, device_id_type=pl.DeviceIdType.MESH)
 
+    loads = [
+        pltpu.make_async_copy(q_hbm, q_buf, in_sem.at[0]),
+        pltpu.make_async_copy(qr_hbm, qr_buf, in_sem.at[1]),
+        pltpu.make_async_copy(o_hbm, o_buf, in_sem.at[2]),
+    ]
+    weights = [
+        pltpu.make_async_copy(wk_hbm, wk_ref, in_sem.at[6]),
+        pltpu.make_async_copy(wv_hbm, wv_ref, in_sem.at[7]),
+    ]
+    early = [
+        pltpu.make_async_copy(len_hbm, len_ref, in_sem.at[8]),
+        pltpu.make_async_copy(lat_hbm, lat_win.at[1], in_sem.at[3]),
+        pltpu.make_async_copy(rope_hbm, rope_buf, in_sem.at[4]),
+        pltpu.make_async_copy(pos_hbm, pos_ref, in_sem.at[5]),
+    ]
+    for copy in weights + early + loads:
+        copy.start()
+    for copy in weights:
+        copy.wait()
+
     half = wk_ref.shape[1] // 2
     for q in range(4):
         rows = (wk_ref, wv_ref)[q // 2][...].astype(F32)
         pack[4 * q : 4 * q + 4, :] = rows[:, (q % 2) * half : (q % 2 + 1) * half]
     zbuf[z] = pack[...].astype(BF16)
+    pl.semaphore_wait(barrier, len(greeted))
+
+    def z_copy(d, slot):
+        return remote(zbuf.at[slot], zbuf.at[slot], z_send.at[d], z_recv.at[d], at(y, x, z_peers[d]))
+
+    for d in range(3):
+        z_copy(d, z).start()
+
     for copy in early:
         copy.wait()
     rope = jnp.transpose(rope_buf[...].astype(F32))
     rot_win[1] = jnp.concatenate([rope, rope], axis=1).astype(BF16)
-
-    pl.semaphore_wait(barrier, len(greeted))
-
-    def z_copy(d, slot):
-        return remote(zbuf.at[slot], zbuf.at[slot], z_send.at[d], z_recv.at[d], at(y, x, z_peers[d]))
-
-    for d in range(3):
-        z_copy(d, z).start()
 
     blocks = [lax.rem(me + tokens + b - 1, tokens) for b in range(3)]
     index = lax.broadcasted_iota(jnp.int32, (1, len_ref.shape[1]), 1)
@@ -137,9 +151,9 @@
         for q in range(4):
             mix[q, 4 * s : 4 * s + 4, :] = piece[4 * q : 4 * q + 4, :]
     for j in range(CHUNKS):
-        lanes = slice((j % 2) * WIDTH, (j % 2 + 1) * WIDTH)
-        wk[j, y, x] = mix[j // 2, :, lanes].astype(BF16)
-        wv[j, y, x] = mix[2 + j // 2, :, lanes].astype(BF16)
+        lanes = slice((j % 4) * WIDTH, (j % 4 + 1) * WIDTH)
+        wk[j, y, x] = mix[j // 4, :, lanes].astype(BF16)
+        wv[j, y, x] = mix[2 + j // 4, :, lanes].astype(BF16)
 
     up, down = at(y_up, x, z), at(y_down, x, z)
     left, right = at(y, x_down, z), at(y, x_up, z)
@@ -156,7 +170,7 @@
         return remote(part, part, g_send.at[n], g_recv.at[n], at(y, x_peers[d], z))
 
     def v_direct(d, offset):
-        part = wv.at[0, y_of(offset), x]
+        part = wv.at[0:DIRECT, y_of(offset), x]
         n = 6 + d
         return remote(part, part, g_send.at[n], g_recv.at[n], at(y_peers[d], x, z))
 
@@ -214,60 +228,65 @@
     def columns(j, width):
         return pl.ds(pl.multiple_of(j * width, width), width)
 
-    def outs(j):
-        plain, rot = columns(j, WIDTH), columns(j, WIDTH // 2)
+    def outs(i):
+        plain, rot = columns(i, HEADS * DIM), columns(i, HEADS * ROPE)
         return [
-            pltpu.make_async_copy(att_buf.at[:, plain], att_hbm.at[:, plain], out_sem.at[j, 0]),
-            pltpu.make_async_copy(dq_buf.at[:, plain], dq_hbm.at[:, plain], out_sem.at[j, 1]),
-            pltpu.make_async_copy(dqr_buf.at[:, rot], dqr_hbm.at[:, rot], out_sem.at[j, 2]),
+            pltpu.make_async_copy(att_buf.at[:, plain], att_hbm.at[:, plain], out_sem.at[i, 0]),
+            pltpu.make_async_copy(dq_buf.at[:, plain], dq_hbm.at[:, plain], out_sem.at[i, 1]),
+            pltpu.make_async_copy(dqr_buf.at[:, rot], dqr_hbm.at[:, rot], out_sem.at[i, 2]),
         ]
 
-    def compute(j):
-        plain, rot_cols = columns(j, WIDTH), columns(j, WIDTH // 2)
+    def both(ref, i):
+        return jnp.concatenate([ref[2 * i + k].reshape(LATENT, WIDTH) for k in range(2)], axis=1)
+
+    def compute(i):
+        plain, rot_cols = columns(i, HEADS * DIM), columns(i, HEADS * ROPE)
+        every = range(HEADS)
+        cols = [slice(e * DIM, (e + 1) * DIM) for e in every]
         window = lat_win[...].reshape(3 * TOK, LATENT)
         rot = rot_win[...].reshape(3 * TOK, 2 * ROPE)
-        key_w = wk[j].reshape(LATENT, WIDTH)
-        value_w = wv[j].reshape(LATENT, WIDTH)
+        key_w = both(wk, i)
         keys = dot(window, key_w, 1, 0).astype(BF16)
-        values = dot(window, value_w, 1, 0).astype(BF16)
-        queries, cots, rots = q_buf[:, plain], o_buf[:, plain], qr_buf[:, rot_cols]
+        queries, rots = q_buf[:, plain], qr_buf[:, rot_cols]
         first = lax.broadcasted_iota(jnp.int32, (TOK, 2 * ROPE), 1) < ROPE
         blank = jnp.zeros((TOK, 2 * ROPE), BF16)
-        key_parts, value_parts, attended, grads, rot_grads = [], [], [], [], []
-        rot_part = None
-        for e in range(4):
-            cols = slice(e * DIM, (e + 1) * DIM)
-            value, cot = values[:, cols], cots[:, cols]
-            r_pair = rots[:, (e // 2) * DIM : (e // 2 + 1) * DIM]
+        key, query = [], []
+        for e in every:
+            r_pair = rots[:, cols[e // 2]]
             r_own = jnp.where(first, r_pair, blank) if e % 2 == 0 else jnp.where(first, blank, r_pair)
-            key_full = jnp.concatenate([keys[:, cols], rot], axis=1)
-            query_full = jnp.concatenate([queries[:, cols], r_own], axis=1)
-            scores = dot(query_full, key_full, 1, 1) * SCALE + bias[...]
-            top = jnp.max(scores, axis=1, keepdims=True)
-            weights = jnp.exp(scores - top)
-            weights = weights * (1.0 / jnp.sum(weights, axis=1, keepdims=True))
-            probs = weights.astype(BF16)
-            out = dot(probs, value, 1, 0).astype(BF16)
-            delta = jnp.sum(cot.astype(F32) * out.astype(F32), axis=1, keepdims=True)
-            prob_grad = dot(cot, value, 1, 1)
-            score_grad = (weights * (prob_grad - delta)).astype(BF16)
-            grad = dot(score_grad, key_full, 1, 0) * SCALE
-            key_side = dot(query_full, score_grad, 0, 0) * SCALE
-            value_parts.append(dot(cot, probs, 0, 0).astype(BF16))
-            key_parts.append(key_side[:DIM].astype(BF16))
-            rot_part = key_side[DIM:] if rot_part is None else rot_part + key_side[DIM:]
-            attended.append(out)
-            grads.append(grad[:, :DIM])
-            rot_grads.append(grad[:, DIM:])
-        att_buf[:, plain] = jnp.concatenate(attended, axis=1)
-        dq_buf[:, plain] = jnp.concatenate(grads, axis=1)
+            key.append(jnp.concatenate([keys[:, cols[e]], rot], axis=1))
+            query.append(jnp.concatenate([queries[:, cols[e]], r_own], axis=1))
+        scores = [dot(query[e], key[e], 1, 1) for e in every]
+        value_w = both(wv, i)
+        values = dot(window, value_w, 1, 0).astype(BF16)
+        value = [values[:, cols[e]] for e in every]
+        cots = o_buf[:, plain]
+        cot = [cots[:, cols[e]] for e in every]
+        mask = bias[...]
+        weights = []
+        for e in every:
+            score = scores[e] * SCALE + mask
+            top = jnp.max(score, axis=1, keepdims=True)
+            weight = jnp.exp(score - top)
+            weights.append(weight * (1.0 / jnp.sum(weight, axis=1, keepdims=True)))
+        prob_grad = [dot(cot[e], value[e], 1, 1) for e in every]
+        probs = [weight.astype(BF16) for weight in weights]
+        out = [dot(probs[e], value[e], 1, 0).astype(BF16) for e in every]
+        value_side = [dot(cot[e], probs[e], 0, 0).astype(BF16) for e in every]
+        delta = [jnp.sum(cot[e].astype(F32) * out[e].astype(F32), axis=1, keepdims=True) for e in every]
+        score_grad = [(weights[e] * (prob_grad[e] - delta[e])).astype(BF16) for e in every]
+        key_side = [dot(query[e], score_grad[e], 0, 0) * SCALE for e in every]
+        grad = [dot(score_grad[e], key[e], 1, 0) * SCALE for e in every]
+        key_part = [side[:DIM].astype(BF16) for side in key_side]
+        att_buf[:, plain] = jnp.concatenate(out, axis=1)
+        dq_buf[:, plain] = jnp.concatenate([g[:, :DIM] for g in grad], axis=1)
         dqr_buf[:, rot_cols] = jnp.concatenate(
-            [jnp.where(first, rot_grads[e], rot_grads[e + 1]) for e in (0, 2)], axis=1
+            [jnp.where(first, grad[e][:, DIM:], grad[e + 1][:, DIM:]) for e in range(0, HEADS, 2)], axis=1
         )
-        back = dot(key_w, jnp.concatenate(key_parts, axis=0), 1, 0)
-        acc[:LATENT] += back + dot(value_w, jnp.concatenate(value_parts, axis=0), 1, 0)
-        acc[LATENT:] += rot_part
-        for copy in outs(j):
+        back = dot(key_w, jnp.concatenate(key_part, axis=0), 1, 0)
+        acc[:LATENT] += back + dot(value_w, jnp.concatenate(value_side, axis=0), 1, 0)
+        acc[LATENT:] += sum(side[DIM:] for side in key_side[1:]) + key_side[0][DIM:]
+        for copy in outs(i):
             copy.start()
 
     def slot(t, carry):
@@ -294,75 +313,69 @@
         for n in reversed(range(1, 3)):
             during(t - V_SLOTS[n], lambda j, n=n: hop(v_x, j, n, 2))
         for g in range(2):
-            once(g, lambda g=g: k_arrive(g))
+            once(K_GROUPS[g][0], lambda g=g: k_arrive(g))
         during(t - K_SLOTS[0], lambda j: hop(k_hop, j, 0, 4))
         once(V_SLOTS[0], v_arrive)
         for n in range(1, 5):
-            once(n - 1, lambda n=n: hop(v_hop, 0, n, 4))
+            once(V_HOPS[n - 1], lambda n=n: hop(v_hop, 0, n, 4))
         during(t - V_SLOTS[0], lambda j: hop(v_x, j, 0, 2))
 
-        last = t - max(K_SLOTS[-1], V_SLOTS[-1])
-
-        @pl.when(last == 0)
+        @pl.when(t == LAST + 1)
         def _():
             for copy in loads:
                 copy.wait()
             for copy in halo:
                 copy.wait_recv()
 
-        @pl.when(last >= 0)
+        @pl.when((t > LAST) & (lax.rem(t - LAST, 2) == 1))
         def _():
-            compute(last)
+            compute(lax.div(t - LAST, 2))
 
         return carry
 
-    lax.fori_loop(0, CHUNKS + max(K_SLOTS[-1], V_SLOTS[-1]), slot, 0)
+    lax.fori_loop(0, CHUNKS + LAST, slot, 0)
 
     acc[LATENT:ROWS] += acc[ROWS:]
-    t1_src[...] = acc[pl.ds(pl.multiple_of((1 - core) * HALF, HALF), HALF)].astype(BF16)
-    step1 = remote(t1_src, t1_dst, t_send.at[0], t_recv.at[0], sibling)
-    step1.start()
-    mine = acc[pl.ds(pl.multiple_of(core * HALF, HALF), HALF)]
-    step1.wait_recv()
-    mine = mine + t1_dst[...].astype(F32)
-    t2_src[0] = mine[:, :TOK].astype(BF16)
-    t2_src[1] = mine[:, 2 * TOK :].astype(BF16)
+    pieces = range(PIECES)
+
+    def rows(owner, p):
+        return pl.ds(pl.multiple_of(owner * HALF + p * PIECE, 16), PIECE)
+
+    step1 = [remote(t1_src.at[p], t1_dst.at[p], t_send.at[p, 0], t_recv.at[p, 0], sibling) for p in pieces]
     step2 = [
-        remote(t2_src.at[0], t2_dst.at[0], t_send.at[1], t_recv.at[1], {"ctx": c_prev}),
-        remote(t2_src.at[1], t2_dst.at[1], t_send.at[2], t_recv.at[2], {"ctx": c_next}),
+        [
+            remote(t2_src.at[p, k], t2_dst.at[p, k], t_send.at[p, 1 + k], t_recv.at[p, 1 + k], {"ctx": target})
+            for k, target in enumerate((c_prev, c_next))
+        ]
+        for p in pieces
     ]
-    for copy in step2:
-        copy.start()
-    for copy in step2:
-        copy.wait_recv()
-    t3_src[...] = (mine[:, TOK : 2 * TOK] + t2_dst[0].astype(F32) + t2_dst[1].astype(F32)).astype(BF16)
-    step3 = remote(t3_src, t3_dst, t_send.at[3], t_recv.at[3], partner)
-    step3.start()
-    step3.wait_recv()
-    t4[core] = t3_src[...].astype(F32) + t3_dst[...].astype(F32)
-    step4 = remote(t4.at[core], t4.at[core], t_send.at[4], t_recv.at[4], sibling)
-    step4.start()
-    other = remote(t4.at[1 - core], t4.at[1 - core], t_send.at[4], t_recv.at[4], sibling)
-    other.wait_recv()
-    whole = t4[...].reshape(ROWS, TOK)
-    dlat_ref[...] = jnp.transpose(whole[:LATENT])
-    drope_ref[...] = whole[LATENT:]
-
-    step1.wait_send()
-    for copy in step2:
-        copy.wait_send()
-    step3.wait_send()
-    step4.wait_send()
+    step3 = [remote(t3_src.at[p], t3_dst.at[p], t_send.at[p, 3], t_recv.at[p, 3], partner) for p in pieces]
+
+    def step4(owner, p):
+        return remote(t4.at[owner, p], t4.at[owner, p], t_send.at[p, 4], t_recv.at[p, 4], sibling)
+
+    for p in pieces:
+        t1_src[p] = acc[rows(1 - core, p)].astype(BF16)
+        step1[p].start()
+    centre = []
+    for p in pieces:
+        step1[p].wait_recv()
+        mine = acc[rows(core, p)] + t1_dst[p].astype(F32)
+        t2_src[p, 0] = mine[:, :TOK].astype(BF16)
+        t2_src[p, 1] = mine[:, 2 * TOK :].astype(BF16)
+        for copy in step2[p]:
+            copy.start()
+        centre.append(mine[:, TOK : 2 * TOK])
+
     for d in range(3):
         z_copy(d, z).wait_send()
     for copy in halo:
         copy.wait_send()
-
     for d in range(NY - 1):
         v_direct(d, 0).wait_send()
-    for d in range(3):
-        k_x(0, d, 0).wait_send()
-        k_x(1, d, 0).wait_send()
+    for g in range(2):
+        for d in range(3):
+            k_x(g, d, 0).wait_send()
     for sign in (1, -1):
         for depth in range(4):
             leave(v_hop, 0, sign, depth).wait_send()
@@ -373,14 +386,37 @@
                 leave(k_hop, j, sign, depth).wait_send()
             for depth in range(2):
                 leave(v_x, j, sign, depth).wait_send()
-        for copy in outs(j):
+        return carry
+
+    lax.fori_loop(0, CHUNKS, drain, 0)
+
+    def drain_outs(i, carry):
+        for copy in outs(i):
             copy.wait()
         return carry
 
-    lax.fori_loop(0, CHUNKS, drain, 0)
-
-
-PARTS = (1, 2, 1, 1, 1)
+    lax.fori_loop(0, STEPS, drain_outs, 0)
+
+    for p in pieces:
+        for copy in step2[p]:
+            copy.wait_recv()
+        t3_src[p] = (centre[p] + t2_dst[p, 0].astype(F32) + t2_dst[p, 1].astype(F32)).astype(BF16)
+        step3[p].start()
+    for p in pieces:
+        step3[p].wait_recv()
+        t4[core, p] = t3_src[p].astype(F32) + t3_dst[p].astype(F32)
+        step4(core, p).start()
+    for p in pieces:
+        step4(1 - core, p).wait_recv()
+    whole = t4[...].reshape(ROWS, TOK)
+    dlat_ref[...] = jnp.transpose(whole[:LATENT])
+    drope_ref[...] = whole[LATENT:]
+    for p in pieces:
+        for copy in [step1[p], *step2[p], step3[p], step4(core, p)]:
+            copy.wait_send()
+
+
+PARTS = (2, 4, 2, 1, 1)
 
 
 def write_out(*refs):
@@ -424,7 +460,7 @@
     results = pl.pallas_call(
         kernel,
         out_shape=outs,
-        in_specs=[hbm, hbm, hbm, hbm, vmem, vmem, hbm, vmem, hbm],
+        in_specs=[hbm] * 9,
         out_specs=(hbm, hbm, hbm, vmem, vmem),
         scratch_shapes=[
             pltpu.VMEM((TOK, cols), BF16),
@@ -432,6 +468,9 @@
             pltpu.VMEM((TOK, cols), BF16),
             pltpu.VMEM((ROPE, TOK), BF16),
             pltpu.VMEM(positions.shape, jnp.int32),
+            pltpu.VMEM(w_key.shape, BF16),
+            pltpu.VMEM(w_value.shape, BF16),
+            pltpu.VMEM(lengths.shape, jnp.int32),
             pltpu.VMEM((TOK, cols), BF16),
             pltpu.VMEM((TOK, cols), F32),
             pltpu.VMEM((TOK, rot_cols), F32),
@@ -444,15 +483,15 @@
             pltpu.VMEM((3, TOK, 2 * ROPE), BF16),
             pltpu.VMEM((TOK, 3 * TOK), F32),
             pltpu.VMEM((LATENT + 2 * ROPE, 3 * TOK), F32),
-            pltpu.VMEM((HALF, 3 * TOK), BF16),
-            pltpu.VMEM((HALF, 3 * TOK), BF16),
-            pltpu.VMEM((2, HALF, TOK), BF16),
-            pltpu.VMEM((2, HALF, TOK), BF16),
-            pltpu.VMEM((HALF, TOK), BF16),
-            pltpu.VMEM((HALF, TOK), BF16),
-            pltpu.VMEM((2, HALF, TOK), F32),
-            dma((6,)),
-            dma((CHUNKS, 3)),
+            pltpu.VMEM((PIECES, PIECE, 3 * TOK), BF16),
+            pltpu.VMEM((PIECES, PIECE, 3 * TOK), BF16),
+            pltpu.VMEM((PIECES, 2, PIECE, TOK), BF16),
+            pltpu.VMEM((PIECES, 2, PIECE, TOK), BF16),
+            pltpu.VMEM((PIECES, PIECE, TOK), BF16),
+            pltpu.VMEM((PIECES, PIECE, TOK), BF16),
+            pltpu.VMEM((2, PIECES, PIECE, TOK), F32),
+            dma((9,)),
+            dma((STEPS, 3)),
             dma((3,)),
             dma((3,)),
             dma((4,)),
@@ -461,8 +500,8 @@
             dma((21,)),
             dma((CHUNKS, 12)),
             dma((CHUNKS, 12)),
-            dma((5,)),
-            dma((5,)),
+            dma((PIECES, 5)),
+            dma((PIECES, 5)),
         ],
         compiler_params=pltpu.CompilerParams(
             collective_id=0, has_side_effects=True, vmem_limit_bytes=VMEM_BYTES

time: 88.4 us -> 81.9 us (0.926)
  Pallas kernels: 87.4 us -> 81.1 us
    pallas_call x1, Pallas kernels: 84.9 us -> 78.6 us  [on_device(): pl.pallas_call(kernel, out_shape=outs, in_specs=[hbm] * 9, out_specs=(hbm...]
where the time goes in v3:
time: 81.9 us; the launch traced here: 81.7 us
  Pallas kernels  81.1 us (99%)
    pallas_call x1, Pallas kernels, on_device(): pl.pallas_call(kernel, out_shape=outs, in_specs=[hbm] * 9, out_specs=(hbm...  78.6 us
    pallas_call x1, Pallas kernels, on_device(): pl.pallas_call(write_out, out_shape=outs, in_specs=[hbm] * len(outs), out...  2.52 us

profile of v3, /device:TPU:1, one launch (start us, length us, event | category | flops | bytes accessed | tf_op | source)
XLA Modules:
  0.0 81.7 jit_solution(13916770132334239136)
XLA Ops:
  0.6 78.6 %latent_attention.1 = (bf16[128,2048]{1,0:T(8,128)(2,1)}, f32[128,2048]{1,0:T(8,128)}, f32[128,1024]{1,0:T(8,128)}, f32[128,512]{1,0:T(8,128)}, f32[64,128]{1,0:T(8,128)}) custom-call(bf16[128,2048]{1,0:T(8,128)(2,1)} %q_hbm.1, bf16[128,1024]{1,0:T(8,128)(2,1)} %qr_hbm.1, bf16[128,512]{1,0:T(8,128)(2,1)} %lat_hbm.1, bf16[64,128]{1,0:T(8,128)(2,1)} %bitcast.6, ...), custom_call_target="tpu_custom_call" | custom-call | flops 4700000256 | bytes 5000000 | tf_op jit(solution)/shard_map/latent_attention/pallas_call | solution.py:460
  79.2 2.5 %write_out.1 = (bf16[128,2048]{1,0:T(8,128)(2,1)}, f32[128,2048]{1,0:T(8,128)}, f32[128,1024]{1,0:T(8,128)}, f32[128,512]{1,0:T(8,128)}, f32[64,128]{1,0:T(8,128)}) custom-call(bf16[128,2048]{1,0:T(8,128)(2,1)} %get-tuple-element.15.refs_0_, f32[128,2048]{1,0:T(8,128)} %get-tuple-element.16.refs_1_, f32[128,1024]{1,0:T(8,128)} %get-tuple-element.17.refs_2_, ...), custom_call_target="tpu_custom_call" | custom-call | tf_op jit(solution)/shard_map/write_out/pallas_call | solution.py:512

commit v4 on v3

--- a/solution.py
+++ b/solution.py
@@ -25,11 +25,11 @@
 HALF = ROWS // 2
 PIECE = HALF // PIECES
 K_SLOTS = (0, 3, 5, 7, 9)
-V_SLOTS = (4, 6, 9)
+V_SLOTS = (3, 6, 8)
 K_GROUPS = ((0, 1), (1, CHUNKS))
-DIRECT = 2
+DIRECT = 3
 V_GROUP = (DIRECT, CHUNKS)
-V_HOPS = (0, 2, 4, 6)
+V_HOPS = (1, 3, 5, 6)
 LAST = max(K_SLOTS[-1], V_SLOTS[-1])
 
 BF16 = jnp.bfloat16
@@ -45,8 +45,8 @@
     att_hbm, dq_hbm, dqr_hbm, dlat_ref, drope_ref,
     q_buf, qr_buf, o_buf, rope_buf, pos_ref, wk_ref, wv_ref, len_ref, att_buf, dq_buf, dqr_buf,
     pack, zbuf, mix, wk, wv, lat_win, rot_win, bias, acc,
-    t1_src, t1_dst, t2_src, t2_dst, t3_src, t3_dst, t4,
-    in_sem, out_sem, z_send, z_recv, h_send, h_recv, g_send, g_recv, c_send, c_recv, t_send, t_recv,
+    t1_src, t1_dst, t2_src, t2_dst, w_dst, t3_src, t3_dst, t4,
+    in_sem, out_sem, z_send, z_recv, h_send, h_recv, g_send, g_recv, c_send, c_recv, t_send, t_recv, w_send, w_recv,
 ):
     me = lax.axis_index("ctx")
     head = lax.axis_index("head")
@@ -68,12 +68,16 @@
     c_next, c_prev = lax.rem(me + 1, tokens), lax.rem(me + tokens - 1, tokens)
     sibling = {"head": z_hi * 2 + (1 - core)}
     partner = {"head": (1 - z_hi) * 2 + core}
+    first_z, last_z = z == 0, z == NZ - 1
 
     def remote(src, dst, send, recv, device):
         return pltpu.make_async_remote_copy(
             src_ref=src, dst_ref=dst, send_sem=send, recv_sem=recv,
             device_id=device, device_id_type=pl.DeviceIdType.MESH,
         )
+
+    t2_dst[...] = jnp.zeros_like(t2_dst)
+    w_dst[...] = jnp.zeros_like(w_dst)
 
     barrier = pltpu.get_barrier_semaphore()
     greeted = (
@@ -81,6 +85,7 @@
         + [at(y, p, z) for p in x_peers]
         + [at(p, x, z) for p in y_peers]
         + [{"ctx": c_next}, {"ctx": c_prev}, sibling, partner]
+        + [{"ctx": c_next, **partner}, {"ctx": c_prev, **partner}]
     )
     for device in greeted:
         pl.semaphore_signal(barrier, inc=1, device_id=device, device_id_type=pl.DeviceIdType.MESH)
@@ -349,6 +354,18 @@
         ]
         for p in pieces
     ]
+    far = [
+        [
+            [
+                remote(t2_src.at[p, k], w_dst.at[p, n], w_send.at[p, n], w_recv.at[p, n], {"ctx": target, **half_of})
+                for n, half_of in ((1, partner), (0, {}))
+            ]
+            for k, target in enumerate((c_prev, c_next))
+        ]
+        for p in pieces
+    ]
+    ends = (first_z, last_z)
+
     step3 = [remote(t3_src.at[p], t3_dst.at[p], t_send.at[p, 3], t_recv.at[p, 3], partner) for p in pieces]
 
     def step4(owner, p):
@@ -363,8 +380,14 @@
         mine = acc[rows(core, p)] + t1_dst[p].astype(F32)
         t2_src[p, 0] = mine[:, :TOK].astype(BF16)
         t2_src[p, 1] = mine[:, 2 * TOK :].astype(BF16)
-        for copy in step2[p]:
-            copy.start()
+        for k in range(2):
+            pl.when(jnp.logical_not(ends[k]))(step2[p][k].start)
+
+            @pl.when(ends[k])
+            def _(p=p, k=k):
+                for copy in far[p][k]:
+                    copy.start()
+
         centre.append(mine[:, TOK : 2 * TOK])
 
     for d in range(3):
@@ -398,13 +421,20 @@
     lax.fori_loop(0, STEPS, drain_outs, 0)
 
     for p in pieces:
-        for copy in step2[p]:
-            copy.wait_recv()
+        for k in range(2):
+            pl.when(jnp.logical_not(ends[1 - k]))(step2[p][k].wait_recv)
         t3_src[p] = (centre[p] + t2_dst[p, 0].astype(F32) + t2_dst[p, 1].astype(F32)).astype(BF16)
         step3[p].start()
     for p in pieces:
         step3[p].wait_recv()
-        t4[core, p] = t3_src[p].astype(F32) + t3_dst[p].astype(F32)
+
+        @pl.when(first_z | last_z)
+        def _(p=p):
+            for copy in far[p][0]:
+                copy.wait_recv()
+
+        near = t3_src[p].astype(F32) + t3_dst[p].astype(F32)
+        t4[core, p] = near + (w_dst[p, 0].astype(F32) + w_dst[p, 1].astype(F32))
         step4(core, p).start()
     for p in pieces:
         step4(1 - core, p).wait_recv()
@@ -412,8 +442,15 @@
     dlat_ref[...] = jnp.transpose(whole[:LATENT])
     drope_ref[...] = whole[LATENT:]
     for p in pieces:
-        for copy in [step1[p], *step2[p], step3[p], step4(core, p)]:
+        for copy in [step1[p], step3[p], step4(core, p)]:
             copy.wait_send()
+        for k in range(2):
+            pl.when(jnp.logical_not(ends[k]))(step2[p][k].wait_send)
+
+            @pl.when(ends[k])
+            def _(p=p, k=k):
+                for copy in far[p][k]:
+                    copy.wait_send()
 
 
 PARTS = (2, 4, 2, 1, 1)
@@ -487,6 +524,7 @@
             pltpu.VMEM((PIECES, PIECE, 3 * TOK), BF16),
             pltpu.VMEM((PIECES, 2, PIECE, TOK), BF16),
             pltpu.VMEM((PIECES, 2, PIECE, TOK), BF16),
+            pltpu.VMEM((PIECES, 2, PIECE, TOK), BF16),
             pltpu.VMEM((PIECES, PIECE, TOK), BF16),
             pltpu.VMEM((PIECES, PIECE, TOK), BF16),
             pltpu.VMEM((2, PIECES, PIECE, TOK), F32),
@@ -502,6 +540,8 @@
             dma((CHUNKS, 12)),
             dma((PIECES, 5)),
             dma((PIECES, 5)),
+            dma((PIECES, 2)),
+            dma((PIECES, 2)),
         ],
         compiler_params=pltpu.CompilerParams(
             collective_id=0, has_side_effects=True, vmem_limit_bytes=VMEM_BYTES

time: 81.9 us -> 75.7 us (0.924)
  Pallas kernels: 81.1 us -> 74.9 us
    pallas_call x1, Pallas kernels: 78.6 us -> 72.4 us  [on_device(): pl.pallas_call(kernel, out_shape=outs, in_specs=[hbm] * 9, out_specs=(hbm...]
where the time goes in v4:
time: 75.7 us; the launch traced here: 75.5 us
  Pallas kernels  74.9 us (99%)
    pallas_call x1, Pallas kernels, on_device(): pl.pallas_call(kernel, out_shape=outs, in_specs=[hbm] * 9, out_specs=(hbm...  72.4 us
    pallas_call x1, Pallas kernels, on_device(): pl.pallas_call(write_out, out_shape=outs, in_specs=[hbm] * len(outs), out...  2.52 us

profile of v4, /device:TPU:1, one launch (start us, length us, event | category | flops | bytes accessed | tf_op | source)
XLA Modules:
  0.0 75.5 jit_solution(6971740546094215750)
XLA Ops:
  0.6 72.4 %latent_attention.1 = (bf16[128,2048]{1,0:T(8,128)(2,1)}, f32[128,2048]{1,0:T(8,128)}, f32[128,1024]{1,0:T(8,128)}, f32[128,512]{1,0:T(8,128)}, f32[64,128]{1,0:T(8,128)}) custom-call(bf16[128,2048]{1,0:T(8,128)(2,1)} %q_hbm.1, bf16[128,1024]{1,0:T(8,128)(2,1)} %qr_hbm.1, bf16[128,512]{1,0:T(8,128)(2,1)} %lat_hbm.1, bf16[64,128]{1,0:T(8,128)(2,1)} %bitcast.6, ...), custom_call_target="tpu_custom_call" | custom-call | flops 4700000256 | bytes 5000000 | tf_op jit(solution)/shard_map/latent_attention/pallas_call | solution.py:497
  73.0 2.5 %write_out.1 = (bf16[128,2048]{1,0:T(8,128)(2,1)}, f32[128,2048]{1,0:T(8,128)}, f32[128,1024]{1,0:T(8,128)}, f32[128,512]{1,0:T(8,128)}, f32[64,128]{1,0:T(8,128)}) custom-call(bf16[128,2048]{1,0:T(8,128)(2,1)} %get-tuple-element.15.refs_0_, f32[128,2048]{1,0:T(8,128)} %get-tuple-element.16.refs_1_, f32[128,1024]{1,0:T(8,128)} %get-tuple-element.17.refs_2_, ...), custom_call_target="tpu_custom_call" | custom-call | tf_op jit(solution)/shard_map/write_out/pallas_call | solution.py:552

commit v5 on v4

--- a/solution.py
+++ b/solution.py
@@ -26,7 +26,7 @@
 PIECE = HALF // PIECES
 K_SLOTS = (0, 3, 5, 7, 9)
 V_SLOTS = (3, 6, 8)
-K_GROUPS = ((0, 1), (1, CHUNKS))
+K_GROUPS = ((0, 2), (2, CHUNKS))
 DIRECT = 3
 V_GROUP = (DIRECT, CHUNKS)
 V_HOPS = (1, 3, 5, 6)
@@ -155,10 +155,10 @@
         piece = zbuf[s].astype(F32)
         for q in range(4):
             mix[q, 4 * s : 4 * s + 4, :] = piece[4 * q : 4 * q + 4, :]
-    for j in range(CHUNKS):
-        lanes = slice((j % 4) * WIDTH, (j % 4 + 1) * WIDTH)
-        wk[j, y, x] = mix[j // 4, :, lanes].astype(BF16)
-        wv[j, y, x] = mix[2 + j // 4, :, lanes].astype(BF16)
+    def assemble(target, first, chunks):
+        for j in chunks:
+            lanes = slice((j % 4) * WIDTH, (j % 4 + 1) * WIDTH)
+            target[j, y, x] = mix[first + j // 4, :, lanes].astype(BF16)
 
     up, down = at(y_up, x, z), at(y_down, x, z)
     left, right = at(y, x_down, z), at(y, x_up, z)
@@ -213,12 +213,15 @@
             if n < last:
                 leave(make, j, sign, n).start()
 
+    assemble(wv, 2, range(DIRECT))
     for d in range(NY - 1):
         v_direct(d, 0).start()
     for g in range(2):
+        assemble(wk, 0, range(*K_GROUPS[g]))
         for d in range(3):
             k_x(g, d, 0).start()
         if g == 0:
+            assemble(wv, 2, range(*V_GROUP))
             hop(v_hop, 0, 0, 4)
 
     halo = [

time: 75.7 us -> 75.7 us (level)
  no operation moved by 1% of the time
where the time goes in v5:
time: 75.7 us; the launch traced here: 75.5 us
  Pallas kernels  74.9 us (99%)
    pallas_call x1, Pallas kernels, on_device(): pl.pallas_call(kernel, out_shape=outs, in_specs=[hbm] * 9, out_specs=(hbm...  72.4 us
    pallas_call x1, Pallas kernels, on_device(): pl.pallas_call(write_out, out_shape=outs, in_specs=[hbm] * len(outs), out...  2.52 us

profile of v5, /device:TPU:1, one launch (start us, length us, event | category | flops | bytes accessed | tf_op | source)
XLA Modules:
  0.0 75.5 jit_solution(2159296395131968935)
XLA Ops:
  0.6 72.4 %latent_attention.1 = (bf16[128,2048]{1,0:T(8,128)(2,1)}, f32[128,2048]{1,0:T(8,128)}, f32[128,1024]{1,0:T(8,128)}, f32[128,512]{1,0:T(8,128)}, f32[64,128]{1,0:T(8,128)}) custom-call(bf16[128,2048]{1,0:T(8,128)(2,1)} %q_hbm.1, bf16[128,1024]{1,0:T(8,128)(2,1)} %qr_hbm.1, bf16[128,512]{1,0:T(8,128)(2,1)} %lat_hbm.1, bf16[64,128]{1,0:T(8,128)(2,1)} %bitcast.6, ...), custom_call_target="tpu_custom_call" | custom-call | flops 4700000256 | bytes 5000000 | tf_op jit(solution)/shard_map/latent_attention/pallas_call | solution.py:500
  73.0 2.5 %write_out.1 = (bf16[128,2048]{1,0:T(8,128)(2,1)}, f32[128,2048]{1,0:T(8,128)}, f32[128,1024]{1,0:T(8,128)}, f32[128,512]{1,0:T(8,128)}, f32[64,128]{1,0:T(8,128)}) custom-call(bf16[128,2048]{1,0:T(8,128)(2,1)} %get-tuple-element.15.refs_0_, f32[128,2048]{1,0:T(8,128)} %get-tuple-element.16.refs_1_, f32[128,1024]{1,0:T(8,128)} %get-tuple-element.17.refs_2_, ...), custom_call_target="tpu_custom_call" | custom-call | tf_op jit(solution)/shard_map/write_out/pallas_call | solution.py:555
